TPU v7x, 32 devices: a whole 2x2x4 slice. The times are simulated.
32 devices in a mesh: grid: 8 (over z, x), kpt: 4 (over y, core).
Axes of the slice: x: 2, y: 2, z: 4, core: 2. Of those that a mesh axis runs over, the one named last changes fastest.
Arguments:
- orbitals: bfloat16 [256, 13, 48, 128], P(('grid', 'kpt')), may hold values from -0.19921875 to 0.19921875
- potential: float32 [256, 128], P(('grid', 'kpt')), may hold values from -3 to 1
- batch_pairs: int32 [256, 48, 48], P(('grid', 'kpt')), may hold values from 0 to 255, as said below
- pair_info: int32 [3, 256], replicated, may hold values from 0 to 60, as said below
- mirror: int32 [256], replicated, may hold values from 0 to 255, as said below
- cell_table: int32 [61, 3], replicated, may hold values from -3 to 3, as said below
- kpoints: float32 [4, 3], P('kpt'), may hold values from -0.5 to 0.5
Outputs:
- hamiltonian: float32 [4, 2, 32, 13, 416], P('kpt', None, 'grid')
Inputs may be any that keep to these rules, and one draw needn't show every extreme that they name: Pair n = (g * 4 + c) * 8 + q belongs to grid index g and kpt index c, and its first atom pair_info[0, n] lies in q * 4 to (q + 1) * 4 - 1; pair_info[2, n] is a cell index below 61. mirror is an involution without fixed points; mirror[n] has first atom pair_info[1, n], second atom pair_info[0, n] and cell 61 - 1 - pair_info[2, n]; the mirror of a pair of grid index g and kpt index c belongs to grid index (g + 4) mod 8 and the same kpt index. cell_table[60 - r] = -cell_table[r]; the middle cell is the zero vector. `batch_pairs`: A batch held by grid index g and kpt index c names only pairs of kpt index c and of grid index g - 1, g or g + 1 (mod 8).
All inputs are finite; a program needn't handle non-finite values.
Results may differ from a plain program's by a relative error of at most 0.00093.
Values sent between devices are 32-bit elements; how exact they have to be, the bound alone decides.
A program may use at most 128 MiB of HBM per device.

v0:
```python
import math

import jax
import jax.numpy as jnp
from jax import lax
from jax.sharding import PartitionSpec as P

NAO = 13
ATOM_DEV = 4


two_pi = 2.0 * math.pi


def shifted(value, axis, steps):
    count = lax.axis_size(axis)
    pairs = [(source, (source + steps) % count) for source in range(count)]
    return lax.ppermute(value, axis, pairs)


def integrate(orbitals, potential, batch_pairs, npairs):
    count, width, slots, points = orbitals.shape
    per_turn = 4

    def advance(pair_table, turn):
        start = turn * per_turn
        values = lax.dynamic_slice_in_dim(orbitals, start, per_turn, 0)
        weights = lax.dynamic_slice_in_dim(potential, start, per_turn, 0)
        targets = lax.dynamic_slice_in_dim(batch_pairs, start, per_turn, 0)
        scaled = (values.astype(jnp.float32) * weights[:, None, None, :]).astype(jnp.bfloat16)
        blocks = jnp.einsum("gxap,gybp->xygab", values, scaled, preferred_element_type=jnp.float32)
        blocks = blocks.reshape(width * width, per_turn * slots * slots)
        return (pair_table.at[:, targets.reshape(-1)].add(blocks), None)

    empty = jnp.zeros((width * width, npairs), jnp.float32)
    pair_table, _ = lax.scan(advance, empty, jnp.arange(count // per_turn, dtype=jnp.int32))
    return pair_table


def flip_blocks(blocks):
    return blocks.reshape(NAO, NAO, -1).transpose(1, 0, 2).reshape(NAO * NAO, -1)


def phase_sum(blocks, pair_ids, pair_info, cell_table, kpoints, first_atom, atoms):
    info = jnp.take(pair_info, pair_ids, axis=1)
    cells = jnp.take(cell_table, info[2], axis=0).astype(jnp.float32)
    angle = two_pi * jnp.dot(kpoints, cells.T, precision=lax.Precision.HIGHEST)
    phases = jnp.stack([jnp.cos(angle), jnp.sin(angle)], axis=1)
    row_hot = (
        info[0][:, None] - first_atom == jnp.arange(ATOM_DEV, dtype=jnp.int32)[None, :]
    ).astype(jnp.float32)
    col_hot = (info[1][:, None] == jnp.arange(atoms, dtype=jnp.int32)[None, :]).astype(jnp.float32)
    shaped = blocks.reshape(NAO, NAO, -1)
    weighted = jnp.einsum(
        "ksp,abp,pi->ksiabp", phases, shaped, row_hot, precision=lax.Precision.HIGHEST
    )
    dense = jnp.einsum("ksiabp,pj->ksiajb", weighted, col_hot, precision=lax.Precision.HIGHEST)
    return dense.reshape(kpoints.shape[0], 2, ATOM_DEV, NAO, atoms * NAO)


def on_device(orbitals, potential, batch_pairs, pair_info, mirror, cell_table, kpoints):
    grid_count = lax.axis_size("grid")
    kpt_count = lax.axis_size("kpt")
    npairs = pair_info.shape[1]
    pair_dev = npairs // (grid_count * kpt_count)
    row_pairs = pair_dev // grid_count
    grid_pos = lax.axis_index("grid")
    kpt_pos = lax.axis_index("kpt")
    pair_table = integrate(orbitals, potential, batch_pairs, npairs)

    def holder_block(grid_index):
        start = (grid_index % grid_count * kpt_count + kpt_pos) * pair_dev
        return lax.dynamic_slice_in_dim(pair_table, start, pair_dev, 1)

    own_part = holder_block(grid_pos)
    lower_part = holder_block(grid_pos - 1 + grid_count)
    upper_part = holder_block(grid_pos + 1)
    above = shifted(lower_part, "grid", -1)
    below = shifted(upper_part, "grid", 1)
    held = own_part + above + below
    partner = shifted(held, "grid", grid_count // 2)
    own_ids = (grid_pos * kpt_count + kpt_pos) * pair_dev + jnp.arange(pair_dev, dtype=jnp.int32)
    columns = jnp.take(mirror, own_ids) % pair_dev
    symmetric = 0.5 * (held + flip_blocks(jnp.take(partner, columns, axis=1)))
    routed = lax.all_to_all(symmetric, "grid", split_axis=1, concat_axis=1, tiled=True)
    gathered = lax.all_gather(routed, "kpt", axis=1, tiled=True)
    kpt_axis = jnp.arange(kpt_count, dtype=jnp.int32)[:, None, None]
    grid_axis = jnp.arange(grid_count, dtype=jnp.int32)[None, :, None]
    slot_axis = jnp.arange(row_pairs, dtype=jnp.int32)[None, None, :]
    pair_ids = (
        ((grid_axis * kpt_count + kpt_axis) * grid_count + grid_pos) * row_pairs + slot_axis
    ).reshape(-1)
    atoms = ATOM_DEV * grid_count
    return phase_sum(gathered, pair_ids, pair_info, cell_table, kpoints, grid_pos * ATOM_DEV, atoms)


def solution(mesh):
    return jax.shard_map(
        on_device,
        mesh=mesh,
        in_specs=(
            P(("grid", "kpt"), None, None, None),
            P(("grid", "kpt"), None),
            P(("grid", "kpt"), None, None),
            P(),
            P(),
            P(),
            P("kpt", None),
        ),
        out_specs=P("kpt", None, "grid", None, None),
        check_vma=False,
    )
```

profile of v0, /device:TPU:0, one launch (start us, length us, event | category | flops | bytes accessed | tf_op | source)
XLA Modules:
  0.0 249.5 jit_solution(18117861886366262608)
XLA Ops:
  0.0 0.0 copy-start
  0.0 0.0 copy-start.2
  0.0 0.0 copy-start.3
  0.1 0.0 copy-start.4
  0.1 212.6 %while.10 = (s32[]{:T(128)}, f32[169,256]{0,1:T(8,128)S(1)}, s32[2]{0:T(128)S(1)}, s32[8,48,48]{2,1,0:T(8,128)}, bf16[8,13,48,128]{3,2,1,0:T(8,128)(2,1)}, /*ind...) while((s32[]{:T(128)}, f32[169,256]{0,1:T(8,128)S(1)}, s32[2]{0:T(128)S(1)}, ...), condition=%wide.region_2.3_spmd, body=%wide.region_0.2_spmd.sunk | while | flops 401264640 | bytes 64138432 | solution.py:36
  0.1 0.7 dynamic_slice.45
  1.4 0.7 constant_dynamic-slice_fusion.7
  2.1 9.6 %convolution_bitcast_fusion.4 = f32[13,13,4,48,48]{3,4,0,1,2:T(8,128)} fusion(f32[4,128]{1,0:T(4,128)S(1)} %constant_dynamic-slice_fusion.7, bf16[8,13,48,128]{3,2,1,0:T(8,128)(2,1)} %get-tuple-element.118, s32[]{:T(128)S(6)} %select_n.230), kind=kOutput, calls=%fused_computation.5.clone.1 | convolution fusion | flops 399679488 | bytes 7511040 | tf_op jit(solution)/shard_map/while/body/eval_jaxpr/gxap,gybp->xygab/dot_general | solution.py:31
  11.6 18.6 %copy.40 = f32[13,13,4,48,48]{4,3,2,1,0:T(8,128)} copy(f32[13,13,4,48,48]{3,4,0,1,2:T(8,128)} %convolution_bitcast_fusion.4) | data formatting | bytes 12460032 | tf_op jit(solution)/shard_map/while/body/eval_jaxpr/gxap,gybp->xygab/transpose | solution.py:31
  30.2 17.1 %reshape.336 = f32[169,9216]{1,0:T(8,128)} reshape(f32[13,13,4,48,48]{4,3,2,1,0:T(8,128)} %copy.40) | data formatting | bytes 12460032 | tf_op jit(solution)/shard_map/while/body/eval_jaxpr/reshape | solution.py:32
  47.3 0.0 copy-start.1
  47.3 8.7 %copy.41 = f32[9216,169]{1,0:T(8,128)} copy(f32[9216,169]{0,1:T(8,128)} %bitcast.101) | data formatting | bytes 12460032 | tf_op jit(solution)/shard_map/while/body/eval_jaxpr/reshape | solution.py:32
  56.0 0.0 copy-done.1
  56.0 0.1 reshape.335
  56.2 50.2 %scatter_fusion = f32[169,256]{0,1:T(8,128)S(1)} fusion(f32[169,256]{0,1:T(8,128)S(1)} %get-tuple-element.105, s32[9216]{0:T(1024)S(1)} %bitcast.102, f32[9216,169]{1,0:T(8,128)} %copy.41), kind=kCustom, calls=%fused_computation.4.clone.1 | custom fusion | flops 1557504 | bytes 18726912 | tf_op jit(solution)/shard_map/while/body/eval_jaxpr/scatter-add | solution.py:33
  106.4 0.7 dynamic_slice.45
  107.7 0.7 constant_dynamic-slice_fusion.7
  108.4 9.4 %convolution_bitcast_fusion.4 = f32[13,13,4,48,48]{3,4,0,1,2:T(8,128)} fusion(f32[4,128]{1,0:T(4,128)S(1)} %constant_dynamic-slice_fusion.7, bf16[8,13,48,128]{3,2,1,0:T(8,128)(2,1)} %get-tuple-element.118, s32[]{:T(128)S(6)} %select_n.230), kind=kOutput, calls=%fused_computation.5.clone.1 | convolution fusion | flops 399679488 | bytes 7511040 | tf_op jit(solution)/shard_map/while/body/eval_jaxpr/gxap,gybp->xygab/dot_general | solution.py:31
  117.8 18.6 %copy.40 = f32[13,13,4,48,48]{4,3,2,1,0:T(8,128)} copy(f32[13,13,4,48,48]{3,4,0,1,2:T(8,128)} %convolution_bitcast_fusion.4) | data formatting | bytes 12460032 | tf_op jit(solution)/shard_map/while/body/eval_jaxpr/gxap,gybp->xygab/transpose | solution.py:31
  136.4 17.1 %reshape.336 = f32[169,9216]{1,0:T(8,128)} reshape(f32[13,13,4,48,48]{4,3,2,1,0:T(8,128)} %copy.40) | data formatting | bytes 12460032 | tf_op jit(solution)/shard_map/while/body/eval_jaxpr/reshape | solution.py:32
  153.5 0.0 copy-start.1
  153.5 8.7 %copy.41 = f32[9216,169]{1,0:T(8,128)} copy(f32[9216,169]{0,1:T(8,128)} %bitcast.101) | data formatting | bytes 12460032 | tf_op jit(solution)/shard_map/while/body/eval_jaxpr/reshape | solution.py:32
  162.3 0.0 copy-done.1
  162.3 0.1 reshape.335
  162.5 50.2 %scatter_fusion = f32[169,256]{0,1:T(8,128)S(1)} fusion(f32[169,256]{0,1:T(8,128)S(1)} %get-tuple-element.105, s32[9216]{0:T(1024)S(1)} %bitcast.102, f32[9216,169]{1,0:T(8,128)} %copy.41), kind=kCustom, calls=%fused_computation.4.clone.1 | custom fusion | flops 1557504 | bytes 18726912 | tf_op jit(solution)/shard_map/while/body/eval_jaxpr/scatter-add | solution.py:33
  212.7 6.0 %collective-permute-start = (f32[169,8]{0,1:T(8,128)S(1)}, f32[169,8]{0,1:T(8,128)S(1)}, u32[]{:S(2)}, u32[]{:S(2)}) collective-permute-start(f32[169,8]{0,1:T(8,128)S(1)} %get-tuple-element.53), channel_id=1, source_target_pairs={{0,28},{4,0},{8,4},{12,8},{16,12},{20,16},{24,20},{28,24},{1,29},{... | collective-permute-start | bytes 16232 | tf_op jit(solution)/shard_map/ppermute | solution.py:18
  218.7 0.0 collective-permute-start.1
  218.7 0.0 copy-done
  218.7 0.6 gather_fusion.2
  219.4 0.1 add.259
  219.5 0.1 add.251
  219.6 0.1 add.261
  219.7 0.0 copy-done.2
  219.7 0.1 copy.29
  219.9 0.1 add.253
  219.9 0.6 gather_fusion
  220.5 0.1 select_bitcast_fusion.1
  220.6 0.2 slice_reduce_fusion.1
  220.9 0.0 copy-done.3
  220.9 0.1 copy.30
  221.0 0.6 gather_fusion.1
  221.6 0.0 copy-done.4
  221.6 0.3 cosine_bitcast_fusion
  221.9 0.0 collective-permute-done
  221.9 3.2 %collective-permute-done.1 = f32[169,8]{0,1:T(8,128)S(1)} collective-permute-done((f32[169,8]{0,1:T(8,128)S(1)}, f32[169,8]{0,1:T(8,128)S(1)}, u32[]{:S(2)}, u32[]{:S(2)}) %collective-permute-start.1) | collective-permute-done | bytes 5440 | tf_op jit(solution)/shard_map/ppermute | solution.py:18
  225.0 0.0 collective-permute-start.2
  225.1 4.5 %collective-permute-done.2 = f32[169,8]{0,1:T(8,128)S(1)} collective-permute-done((f32[169,8]{0,1:T(8,128)S(1)}, f32[169,8]{0,1:T(8,128)S(1)}, u32[]{:S(2)}, u32[]{:S(2)}) %collective-permute-start.2) | collective-permute-done | bytes 5440 | tf_op jit(solution)/shard_map/ppermute | solution.py:18
  229.6 0.6 gather_fusion.3
  230.2 0.1 gather.25
  230.2 0.1 select_bitcast_fusion
  230.3 0.1 copy.31
  230.5 0.1 reshape.273
  230.6 0.6 copy.32
  231.2 3.3 %all-to-all-start = ((f32[169,8,1]{0,2,1:T(1,128)}), f32[169,8,1]{0,2,1:T(1,128)S(1)}, u32[]{:S(2)}, u32[]{:S(2)}) async-start(f32[169,8,1]{0,2,1:T(1,128)} %copy.32), calls=%async_computation | async-start | bytes 16384 | tf_op jit(solution)/shard_map/all_to_all | solution.py:85
  234.5 6.4 %all-to-all-done = f32[169,8,1]{0,2,1:T(1,128)S(1)} async-done(((f32[169,8,1]{0,2,1:T(1,128)}), f32[169,8,1]{0,2,1:T(1,128)S(1)}, u32[]{:S(2)}, u32[]{:S(2)}) %all-to-all-start) | async-done | bytes 5440 | tf_op jit(solution)/shard_map/all_to_all | solution.py:85
  241.0 5.2 %all-gather = f32[169,32,1]{0,2,1:T(1,128)S(1)} all-gather(f32[169,8,1]{0,2,1:T(1,128)S(1)} %all-to-all-done), channel_id=2, replica_groups=mesh['grid'=8,'kpt'=4] {'kpt'}, dimensions={1}, use_global_device_ids=true | all-gather | bytes 27040 | tf_op jit(solution)/shard_map/all_gather | solution.py:86
  246.1 0.1 copy.33
  246.3 0.6 convolution_bitcast_fusion.1
  246.9 0.7 copy.34
  247.5 1.9 reshape.277
  (28 shorter events, 0.3 us)
Async XLA Ops:
  0.0 218.7 %copy-start = (s32[256]{0:T(256)S(1)}, s32[256]{0:T(256)}, u32[]{:S(2)}) copy-start(s32[256]{0:T(256)} %param.13) | copy-start | bytes 3076
  0.0 219.7 %copy-start.2 = (s32[3,256]{1,0:T(4,128)S(1)}, s32[3,256]{1,0:T(4,128)}, u32[]{:S(2)}) copy-start(s32[3,256]{1,0:T(4,128)} %param.12) | copy-start | bytes 9220
  0.0 220.8 %copy-start.3 = (s32[61,3]{0,1:T(4,128)S(1)}, s32[61,3]{0,1:T(4,128)}, u32[]{:S(2)}) copy-start(s32[61,3]{0,1:T(4,128)} %param.14) | copy-start | bytes 2200
  0.1 221.5 %copy-start.4 = (f32[1,3]{1,0:T(1,128)S(1)}, f32[1,3]{1,0:T(1,128)}, u32[]{:S(2)}) copy-start(f32[1,3]{1,0:T(1,128)} %param.15) | copy-start | bytes 40
  47.3 8.7 %copy-start.1 = (s32[8,48,48]{2,1,0:T(8,128)S(1)}, s32[8,48,48]{2,1,0:T(8,128)}, u32[]{:S(2)}) copy-start(s32[8,48,48]{2,1,0:T(8,128)} %get-tuple-element.117) | copy-start | bytes 221188 | tf_op jit(solution)/shard_map/while
  153.5 8.7 %copy-start.1 = (s32[8,48,48]{2,1,0:T(8,128)S(1)}, s32[8,48,48]{2,1,0:T(8,128)}, u32[]{:S(2)}) copy-start(s32[8,48,48]{2,1,0:T(8,128)} %get-tuple-element.117) | copy-start | bytes 221188 | tf_op jit(solution)/shard_map/while
  212.7 9.2 %collective-permute-start = (f32[169,8]{0,1:T(8,128)S(1)}, f32[169,8]{0,1:T(8,128)S(1)}, u32[]{:S(2)}, u32[]{:S(2)}) collective-permute-start(f32[169,8]{0,1:T(8,128)S(1)} %get-tuple-element.53), channel_id=1, source_target_pairs={{0,28},{4,0},{8,4},{12,8},{16,12},{20,16},{24,20},{28,24},{1,29},{... | collective-permute-start | bytes 16232 | tf_op jit(solution)/shard_map/ppermute | solution.py:18
  218.7 6.3 %collective-permute-start.1 = (f32[169,8]{0,1:T(8,128)S(1)}, f32[169,8]{0,1:T(8,128)S(1)}, u32[]{:S(2)}, u32[]{:S(2)}) collective-permute-start(f32[169,8]{0,1:T(8,128)S(1)} %get-tuple-element.54), channel_id=1, source_target_pairs={{0,4},{4,8},{8,12},{12,16},{16,20},{20,24},{24,28},{28,0},{1,5},{5... | collective-permute-start | bytes 16232 | tf_op jit(solution)/shard_map/ppermute | solution.py:18
  225.0 4.5 %collective-permute-start.2 = (f32[169,8]{0,1:T(8,128)S(1)}, f32[169,8]{0,1:T(8,128)S(1)}, u32[]{:S(2)}, u32[]{:S(2)}) collective-permute-start(f32[169,8]{0,1:T(8,128)S(1)} %add_add_fusion), channel_id=1, source_target_pairs={{0,16},{4,20},{8,24},{12,28},{16,0},{20,4},{24,8},{28,12},{1,17},{... | collective-permute-start | bytes 16232 | tf_op jit(solution)/shard_map/ppermute | solution.py:18
  231.2 9.8 %all-to-all-start = ((f32[169,8,1]{0,2,1:T(1,128)}), f32[169,8,1]{0,2,1:T(1,128)S(1)}, u32[]{:S(2)}, u32[]{:S(2)}) async-start(f32[169,8,1]{0,2,1:T(1,128)} %copy.32), calls=%async_computation | async-start | bytes 16384 | tf_op jit(solution)/shard_map/all_to_all | solution.py:85
where the time goes:
time: 252 us; the launch traced here: 249 us
  other arithmetic  101 us (40%)
  local copies, waits for them, and re-layouts  98.4 us (39%)
  matrix products  19.8 us (8%)
  waiting for transfers between devices  14.1 us (6%)
  starting transfers between devices  9.37 us (4%)
  blocking collectives  5.18 us (2%)
    scatter-add x2, other arithmetic, advance(): return (pair_table.at[:, targets.reshape(-1)].add(blocks), None)  100 us
    reshape x4, local copies, waits for them, and re-layouts, advance(): blocks = blocks.reshape(width * width, per_turn * slots * slots)  51.6 us
    transpose x2, local copies, waits for them, and re-layouts, advance(): jnp.einsum('gxap,gybp->xygab', values, scaled, preferred_element_type=jnp...  37.2 us
    dot_general x2, matrix products, advance(): jnp.einsum('gxap,gybp->xygab', values, scaled, preferred_element_type=jnp...  19 us
    ppermute x3, waiting for transfers between devices, shifted(): return lax.ppermute(value, axis, pairs)  7.7 us
    all_to_all x1, waiting for transfers between devices, on_device(): lax.all_to_all(symmetric, 'grid', split_axis=1, concat_axis=1, tiled=True)  6.44 us
    ppermute x3, starting transfers between devices, shifted(): return lax.ppermute(value, axis, pairs)  6.03 us
    all_gather x1, blocking collectives, on_device(): gathered = lax.all_gather(routed, 'kpt', axis=1, tiled=True)  5.18 us
  transfers between devices with their start and end apart: 4, of which 3 were waited for; matrix products, arithmetic and copies ran while one was open for 1% of the time, Pallas kernels for 0%

commit v1 on v0

v1 whole, which is shorter than its diff:
```python
import functools
import math

import jax
import jax.numpy as jnp
from jax import lax
from jax.experimental import pallas as pl
from jax.experimental.pallas import tpu as pltpu
from jax.sharding import PartitionSpec as P

NAO = 13
XP = 16
HALF = 7
CP = 64
ATOM_DEV = 4
A_STEP = 8

two_pi = 2.0 * math.pi
NT = (((1,), (1,)), ((), ()))


def integrate_kernel(ids_ref, orb_ref, pot_ref, pairs_ref, out_ref, rows_f32, left, right, codes, acc):
    step = pl.program_id(0)
    _, width, slots, points = orb_ref.shape

    @pl.when(step == 0)
    def _():
        rows_f32[...] = jnp.zeros_like(rows_f32)
        right[...] = jnp.zeros_like(right)
        codes[...] = jnp.full_like(codes, -1)
        acc[...] = jnp.zeros_like(acc)

    weight = pot_ref[0]
    for y in range(width):
        vals = orb_ref[0, y].astype(jnp.float32)
        base = (y % HALF) * 128 + (y // HALF) * CP
        right[base : base + slots, :] = (vals * weight).astype(jnp.bfloat16)
        rows_f32[y * slots : (y + 1) * slots, :] = vals
    for a in range(slots):
        left[a * XP : (a + 1) * XP, :] = rows_f32[pl.ds(a, XP, stride=slots), :].astype(jnp.bfloat16)
    pairs = pairs_ref[0]
    codes[:, 0:slots] = pairs * 2
    codes[:, CP : CP + slots] = pairs * 2 + 1
    ids = ids_ref[...]
    for a0 in range(0, slots, A_STEP):
        prod = lax.dot_general(
            left[a0 * XP : (a0 + A_STEP) * XP, :], right[...], NT, preferred_element_type=jnp.float32
        )
        high = prod.astype(jnp.bfloat16)
        low = (prod - high.astype(jnp.float32)).astype(jnp.bfloat16)
        cols, hots = [], []
        for a in range(A_STEP):
            parts = [
                part[a * XP : (a + 1) * XP, yp * 128 : (yp + 1) * 128]
                for part in (high, low)
                for yp in range(HALF)
            ]
            cols.append(jnp.concatenate(parts, axis=0))
            hots.append(
                (codes[a0 + a : a0 + a + 1, :] == ids).astype(jnp.float32).astype(jnp.bfloat16)
            )
        acc[...] += lax.dot_general(
            jnp.concatenate(cols, axis=1),
            jnp.concatenate(hots, axis=1),
            NT,
            preferred_element_type=jnp.float32,
        )

    @pl.when(step == pl.num_programs(0) - 1)
    def _():
        half = HALF * XP
        out_ref[...] = acc[:half, :] + acc[half:, :]


def integrate(ids, orbitals, potential, batch_pairs):
    count, width, slots, points = orbitals.shape
    ncol = ids.shape[0]
    return pl.pallas_call(
        integrate_kernel,
        grid=(count,),
        out_shape=jax.ShapeDtypeStruct((HALF * XP, ncol), jnp.float32),
        in_specs=[
            pl.BlockSpec((ncol, 128), lambda b: (0, 0)),
            pl.BlockSpec((1, width, slots, points), lambda b: (b, 0, 0, 0)),
            pl.BlockSpec((1, 1, points), lambda b: (b, 0, 0)),
            pl.BlockSpec((1, slots, slots), lambda b: (b, 0, 0)),
        ],
        out_specs=pl.BlockSpec((HALF * XP, ncol), lambda b: (0, 0)),
        scratch_shapes=[
            pltpu.VMEM((XP * slots, points), jnp.float32),
            pltpu.VMEM((slots * XP, points), jnp.bfloat16),
            pltpu.VMEM((HALF * 128, points), jnp.bfloat16),
            pltpu.VMEM((slots, 128), jnp.int32),
            pltpu.VMEM((2 * HALF * XP, ncol), jnp.float32),
        ],
        compiler_params=pltpu.CompilerParams(
            dimension_semantics=("arbitrary",), vmem_limit_bytes=48 * 1024 * 1024
        ),
    )(ids, orbitals, potential.reshape(count, 1, points), batch_pairs)


def phase_sum(blocks, info, cell_table, kpoints, first_atom, atoms):
    cells = jnp.take(cell_table, info[2], axis=0).astype(jnp.float32)
    angle = two_pi * jnp.dot(kpoints, cells.T, precision=lax.Precision.HIGHEST)
    phases = jnp.stack([jnp.cos(angle), jnp.sin(angle)], axis=1)
    row_hot = (
        info[0][:, None] - first_atom == jnp.arange(ATOM_DEV, dtype=jnp.int32)[None, :]
    ).astype(jnp.float32)
    col_hot = (info[1][:, None] == jnp.arange(atoms, dtype=jnp.int32)[None, :]).astype(jnp.float32)
    shaped = blocks.reshape(NAO, NAO, -1)
    weighted = jnp.einsum(
        "ksp,abp,pi->ksiabp", phases, shaped, row_hot, precision=lax.Precision.HIGHEST
    )
    dense = jnp.einsum("ksiabp,pj->ksiajb", weighted, col_hot, precision=lax.Precision.HIGHEST)
    return dense.reshape(kpoints.shape[0], 2, ATOM_DEV, NAO, atoms * NAO)


def on_device(orbitals, potential, batch_pairs, pair_info, mirror, cell_table, kpoints):
    grid_count = lax.axis_size("grid")
    kpt_count = lax.axis_size("kpt")
    npairs = pair_info.shape[1]
    pair_dev = npairs // (grid_count * kpt_count)
    row_pairs = pair_dev // grid_count
    grid_pos = lax.axis_index("grid")
    kpt_pos = lax.axis_index("kpt")
    half = grid_count // 2

    shift = jnp.arange(-1, 2, dtype=jnp.int32)[:, None]
    slot = jnp.arange(pair_dev, dtype=jnp.int32)[None, :]

    def pair_id(offset):
        holder = (grid_pos + shift + offset + grid_count) % grid_count
        return (holder * kpt_count + kpt_pos) * pair_dev + slot

    ids = jnp.stack([pair_id(0), jnp.take(mirror, pair_id(half))])
    ids = ids[:, :, None, :] * 2 + jnp.arange(2, dtype=jnp.int32)[None, None, :, None]
    ids = jnp.broadcast_to(ids.reshape(-1, 1), (12 * pair_dev, 128))
    table = integrate(ids, orbitals, potential, batch_pairs)
    table = table.reshape(HALF, XP, 2, 3, 2, grid_count, row_pairs)[:, :NAO]
    send = table.transpose(5, 2, 3, 6, 4, 0, 1)
    got = lax.all_to_all(send, "grid", split_axis=0, concat_axis=0, tiled=True)
    direct = sum(jnp.roll(got[:, 0, s], s - 1, axis=0) for s in range(3))
    mirrored = sum(jnp.roll(got[:, 1, s], s - 1 + half, axis=0) for s in range(3))

    def square(value):
        return value.reshape(grid_count, row_pairs, 2 * HALF, NAO)[:, :, :NAO]

    sym = 0.5 * (square(direct).transpose(3, 2, 0, 1) + square(mirrored).transpose(2, 3, 0, 1))
    gathered = lax.all_gather(sym.reshape(NAO * NAO, 1, -1), "kpt", axis=1, tiled=True)
    info = pair_info.reshape(3, grid_count, kpt_count, grid_count, row_pairs)
    info = lax.dynamic_slice_in_dim(info, grid_pos, 1, 3)[:, :, :, 0]
    info = info.transpose(0, 2, 1, 3).reshape(3, -1)
    atoms = ATOM_DEV * grid_count
    return phase_sum(
        gathered.reshape(NAO * NAO, -1), info, cell_table, kpoints, grid_pos * ATOM_DEV, atoms
    )


def solution(mesh):
    return jax.shard_map(
        on_device,
        mesh=mesh,
        in_specs=(
            P(("grid", "kpt"), None, None, None),
            P(("grid", "kpt"), None),
            P(("grid", "kpt"), None, None),
            P(),
            P(),
            P(),
            P("kpt", None),
        ),
        out_specs=P("kpt", None, "grid", None, None),
        check_vma=False,
    )
```

time: 252 us -> 44.9 us (0.18)
  other arithmetic: 101 us -> 1.12 us
  local copies, waits for them, and re-layouts: 98.4 us -> 9.18 us
  matrix products: 19.8 us -> 0.83 us
  Pallas kernels: 0 us -> 15.7 us
  waiting for transfers between devices: 14.1 us -> 4.97 us
    scatter-add x2 -> x0, other arithmetic: 100 us -> none  [advance(): return (pair_table.at[:, targets.reshape(-1)].add(blocks), None)]
    reshape x8 -> x3, local copies, waits for them, and re-layouts: 52 us -> 0.34 us  [the longest x1 0.15 us: on_device(): table = table.reshape(HALF, XP, 2, 3, 2, grid_count, row_pairs)[:, :NAO]]
    transpose x3 -> x2, local copies, waits for them, and re-layouts: 37.3 us -> 0.3 us  [on_device(): send = table.transpose(5, 2, 3, 6, 4, 0, 1)]
    dot_general x2 -> x0, matrix products: 19 us -> none  [advance(): jnp.einsum('gxap,gybp->xygab', values, scaled, preferred_element_type=jnp...]
    pallas_call x0 -> x1, Pallas kernels: none -> 15.7 us  [integrate(): pl.pallas_call(integrate_kernel, grid=(count,), out_shape=jax.ShapeDtypeS...]
    ppermute x3 -> x0, waiting for transfers between devices: 7.7 us -> none  [shifted(): return lax.ppermute(value, axis, pairs)]
    ppermute x3 -> x0, starting transfers between devices: 6.03 us -> none  [shifted(): return lax.ppermute(value, axis, pairs)]
    all_to_all x1, starting transfers between devices: 3.33 us -> 7.25 us  [on_device(): got = lax.all_to_all(send, 'grid', split_axis=0, concat_axis=0, tiled=True)]
  transfers between devices with their start and end apart: 4 -> 1, of which waited for: 3 -> 1; matrix products, arithmetic and copies ran while one was open for 1% -> 4% of each run, Pallas kernels for 0% -> 0%
where the time goes in v1:
time: 44.9 us; the launch traced here: 44.6 us
  Pallas kernels  15.7 us (35%)
  local copies, waits for them, and re-layouts  9.18 us (20%)
  starting transfers between devices  7.25 us (16%)
  blocking collectives  5.19 us (12%)
  waiting for transfers between devices  4.97 us (11%)
  other arithmetic  1.12 us (2%)
  matrix products  0.83 us (2%)
    pallas_call x1, Pallas kernels, integrate(): pl.pallas_call(integrate_kernel, grid=(count,), out_shape=jax.ShapeDtypeS...  15.7 us
    all_to_all x1, starting transfers between devices, on_device(): got = lax.all_to_all(send, 'grid', split_axis=0, concat_axis=0, tiled=True)  7.25 us
    all_gather x1, blocking collectives, on_device(): lax.all_gather(sym.reshape(NAO * NAO, 1, -1), 'kpt', axis=1, tiled=True)  5.19 us
    all_to_all x1, waiting for transfers between devices, on_device(): got = lax.all_to_all(send, 'grid', split_axis=0, concat_axis=0, tiled=True)  4.97 us
    unnamed x19, local copies, waits for them, and re-layouts  2.13 us
    reshape x1, local copies, waits for them, and re-layouts, phase_sum(): return dense.reshape(kpoints.shape[0], 2, ATOM_DEV, NAO, atoms * NAO)  1.93 us
  transfers between devices with their start and end apart: 1, of which 1 were waited for; matrix products, arithmetic and copies ran while one was open for 4% of the time, Pallas kernels for 0%

profile of v1, /device:TPU:0, one launch (start us, length us, event | category | flops | bytes accessed | tf_op | source)
XLA Modules:
  0.0 44.6 jit_solution(13940558315653766190)
XLA Ops:
  0.0 0.0 copy-start
  0.0 0.0 copy-start.2
  0.0 0.0 copy-start.3
  0.0 0.0 copy-start.1
  0.0 0.1 iota_add_fusion.1
  0.1 0.1 compare_select_fusion
  0.2 0.1 reshape.541
  0.3 0.4 copy-done
  0.7 0.7 %gather_fusion.1 = s32[24]{0:T(128)S(1)} fusion(s32[256]{0:T(256)S(1)} %copy-done, s32[1024]{0:T(1024)S(1)} %pad_clamp_fusion), kind=kCustom, calls=%fused_computation.1 | custom fusion | bytes 288 | tf_op jit(solution)/shard_map/jit(_take)/gather | solution.py:135
  1.4 0.1 gather.12
  1.5 0.1 fusion.23
  1.6 0.1 add.295
  1.7 0.1 broadcast_in_dim.16.ids_ref
  1.7 0.0 copy-done.2
  1.7 0.0 copy-done.3
  1.8 0.0 copy-done.1
  1.8 0.0 copy-start.4
  1.8 15.7 %shard_map.73 = f32[112,96]{1,0:T(8,128)S(1)} custom-call(s32[96,128]{1,0:T(8,128)S(1)} %broadcast_in_dim.16.ids_ref, bf16[8,13,48,128]{3,2,1,0:T(8,128)(2,1)S(1)} %copy-done.1, f32[8,1,128]{2,1,0:T(1,128)S(1)} %bitcast.94, s32[8,48,48]{2,1,0:T(8,128)S(1)} %copy-done.2), custom_call_target="tpu_custom_call" | custom-call | tf_op jit(solution)/shard_map/pallas_call | solution.py:78
  17.5 0.0 copy-start.5
  17.5 0.0 copy-start.6
  17.5 0.1 copy.80
  17.6 0.1 reshape.527
  17.8 0.3 copy.111
  18.1 1.0 %reshape.552 = f32[8,1,1092]{2,1,0:T(1,128)} reshape(f32[8,2,3,1,7,2,13]{6,5,4,3,2,1,0:T(2,128)S(1)} %bitcast.101) | data formatting | bytes 69888
  19.1 7.3 %all-to-all-start = ((f32[8,1,1092]{2,1,0:T(1,128)}), f32[8,1,1092]{2,1,0:T(1,128)S(1)}, u32[]{:S(2)}, u32[]{:S(2)}) async-start(f32[8,1,1092]{2,1,0:T(1,128)} %reshape.552), calls=%async_computation | async-start | bytes 73728 | tf_op jit(solution)/shard_map/all_to_all | solution.py:141
  26.3 0.0 copy-done.4
  26.3 0.1 reshape.523
  26.4 0.1 constant_dynamic-slice_fusion
  26.5 0.1 copy.108
  26.7 0.1 squeeze.18
  26.8 0.1 squeeze.17
  26.8 0.0 copy-done.5
  26.8 0.1 copy.79
  27.0 0.1 sub.16
  27.1 0.6 %gather_fusion = s32[32,3]{1,0:T(8,128)S(1)} fusion(s32[61,3]{1,0:T(8,128)S(1)} %copy.79, s32[1024]{0:T(1024)S(1)} %pad_clamp_fusion.1), kind=kCustom, calls=%fused_computation | custom fusion | bytes 896 | tf_op jit(solution)/shard_map/jit(_take)/gather | solution.py:103
  27.7 0.0 copy-done.6
  27.7 0.3 cosine_bitcast_fusion
  28.0 0.1 eq.31
  28.1 5.0 %all-to-all-done = f32[8,1,1092]{2,1,0:T(1,128)S(1)} async-done(((f32[8,1,1092]{2,1,0:T(1,128)}), f32[8,1,1092]{2,1,0:T(1,128)S(1)}, u32[]{:S(2)}, u32[]{:S(2)}) %all-to-all-start) | async-done | bytes 34976 | tf_op jit(solution)/shard_map/all_to_all | solution.py:141
  33.0 0.5 %broadcast.327 = f32[]{:T(128)} broadcast(f32[]{:T(128)} %constant.143), dimensions={} | broadcast | bytes 8 | tf_op jit(solution)/shard_map/all_to_all | solution.py:141
  33.5 0.7 %reduce = f32[8,1092]{1,0:T(8,128)S(1)} reduce(f32[8,1,1092]{2,1,0:T(1,128)S(1)} %all-to-all-done, f32[]{:T(128)} %broadcast.327), dimensions={1}, to_apply=%all_to_all.3.reduce_sub_computation | reduce | bytes 69892 | tf_op jit(solution)/shard_map/all_to_all | solution.py:141
  34.3 0.3 reshape.553
  34.7 0.1 copy.85
  34.8 0.1 copy.90
  35.0 0.1 copy.109
  35.2 0.1 copy.82
  35.3 0.1 copy.84
  35.5 0.1 copy.89
  35.6 0.1 copy.91
  35.7 0.1 fusion.8
  35.8 0.1 reshape.528
  35.9 5.2 %all_gather.3 = f32[169,4,8]{0,2,1:T(8,128)S(1)} all-gather(f32[169,1,8]{0,2,1:T(8,128)S(1)} %reshape.528), channel_id=1, replica_groups=mesh['grid'=8,'kpt'=4] {'kpt'}, dimensions={1}, use_global_device_ids=true | all-gather | bytes 27040 | tf_op jit(solution)/shard_map/all_gather | solution.py:149
  41.1 0.1 reshape_reshape.5
  41.3 0.2 copy.105
  41.4 0.6 %convolution_bitcast_fusion = f32[1,2,4,13,32,13]{4,5,3,2,1,0:T(8,128)S(1)} fusion(f32[32,13,13]{0,2,1:T(8,128)S(1)} %copy.105, f32[32,4,2]{0,1,2:T(4,128)S(1)} %broadcast_multiply_fusion, s32[32]{0:T(128)S(1)} %eq.31), kind=kOutput, calls=%fused_computation.2 | convolution fusion | flops 16657664 | bytes 195840 | tf_op jit(solution)/shard_map/ksiabp,pj->ksiajb/dot_general | solution.py:114
  42.0 0.7 %copy.106 = f32[1,2,4,13,32,13]{5,4,2,3,1,0:T(8,128)S(1)} copy(f32[1,2,4,13,32,13]{4,5,3,2,1,0:T(8,128)S(1)} %convolution_bitcast_fusion) | data formatting | bytes 346112 | tf_op jit(solution)/shard_map/ksiabp,pj->ksiajb/transpose | solution.py:114
  42.7 1.9 %reshape.530 = f32[1,2,4,13,416]{4,2,3,1,0:T(4,128)} reshape(f32[1,2,4,13,32,13]{5,4,2,3,1,0:T(8,128)S(1)} %copy.106) | data formatting | bytes 346112 | tf_op jit(solution)/shard_map/reshape | solution.py:115
  (33 shorter events, 0.4 us)
Async XLA Ops:
  0.0 0.7 %copy-start = (s32[256]{0:T(256)S(1)}, s32[256]{0:T(256)}, u32[]{:S(2)}) copy-start(s32[256]{0:T(256)} %param.11) | copy-start | bytes 3076
  0.0 1.7 %copy-start.2 = (s32[8,48,48]{2,1,0:T(8,128)S(1)}, s32[8,48,48]{2,1,0:T(8,128)}, u32[]{:S(2)}) copy-start(s32[8,48,48]{2,1,0:T(8,128)} %pairs_ref.1) | copy-start | bytes 221188
  0.0 1.7 %copy-start.3 = (f32[8,128]{1,0:T(8,128)S(1)}, f32[8,128]{1,0:T(8,128)}, u32[]{:S(2)}) copy-start(f32[8,128]{1,0:T(8,128)} %param.8) | copy-start | bytes 12292
  0.0 1.7 %copy-start.1 = (bf16[8,13,48,128]{3,2,1,0:T(8,128)(2,1)S(1)}, bf16[8,13,48,128]{3,2,1,0:T(8,128)(2,1)}, u32[]{:S(2)}) copy-start(bf16[8,13,48,128]{3,2,1,0:T(8,128)(2,1)} %orb_ref.1) | copy-start | bytes 3833860
  1.8 24.5 %copy-start.4 = (s32[3,256]{1,0:T(4,128)S(1)}, s32[3,256]{1,0:T(4,128)}, u32[]{:S(2)}) copy-start(s32[3,256]{1,0:T(4,128)} %param.10) | copy-start | bytes 9220
  17.5 9.4 %copy-start.5 = (s32[61,3]{0,1:T(4,128)S(1)}, s32[61,3]{0,1:T(4,128)}, u32[]{:S(2)}) copy-start(s32[61,3]{0,1:T(4,128)} %param.12) | copy-start | bytes 2200
  17.5 10.2 %copy-start.6 = (f32[1,3]{1,0:T(1,128)S(1)}, f32[1,3]{1,0:T(1,128)}, u32[]{:S(2)}) copy-start(f32[1,3]{1,0:T(1,128)} %param.13) | copy-start | bytes 40
  19.1 14.0 %all-to-all-start = ((f32[8,1,1092]{2,1,0:T(1,128)}), f32[8,1,1092]{2,1,0:T(1,128)S(1)}, u32[]{:S(2)}, u32[]{:S(2)}) async-start(f32[8,1,1092]{2,1,0:T(1,128)} %reshape.552), calls=%async_computation | async-start | bytes 73728 | tf_op jit(solution)/shard_map/all_to_all | solution.py:141

commit v2 on v1

--- a/solution.py
+++ b/solution.py
@@ -16,10 +16,13 @@
 A_STEP = 8
 
 two_pi = 2.0 * math.pi
+MESH = pl.DeviceIdType.MESH
 NT = (((1,), (1,)), ((), ()))
 
 
-def integrate_kernel(ids_ref, orb_ref, pot_ref, pairs_ref, out_ref, rows_f32, left, right, codes, acc):
+def integrate_kernel(
+    ids_ref, orb_ref, pot_ref, pairs_ref, out_ref, rows_f32, left, right, codes, acc, turned
+):
     step = pl.program_id(0)
     _, width, slots, points = orb_ref.shape
 
@@ -69,7 +72,11 @@
     @pl.when(step == pl.num_programs(0) - 1)
     def _():
         half = HALF * XP
-        out_ref[...] = acc[:half, :] + acc[half:, :]
+        out_ref[...] = jnp.zeros_like(out_ref)
+        turned[:, 0:half] = jnp.transpose(acc[:half, :] + acc[half:, :])
+        pair_dev = out_ref.shape[0]
+        for q in range(pair_dev):
+            out_ref[q, 0:12, 0:half] = turned[pl.ds(q, 12, stride=pair_dev), 0:half]
 
 
 def integrate(ids, orbitals, potential, batch_pairs):
@@ -78,20 +85,21 @@
     return pl.pallas_call(
         integrate_kernel,
         grid=(count,),
-        out_shape=jax.ShapeDtypeStruct((HALF * XP, ncol), jnp.float32),
+        out_shape=jax.ShapeDtypeStruct((ncol // 12, XP, 128), jnp.float32),
         in_specs=[
             pl.BlockSpec((ncol, 128), lambda b: (0, 0)),
             pl.BlockSpec((1, width, slots, points), lambda b: (b, 0, 0, 0)),
             pl.BlockSpec((1, 1, points), lambda b: (b, 0, 0)),
             pl.BlockSpec((1, slots, slots), lambda b: (b, 0, 0)),
         ],
-        out_specs=pl.BlockSpec((HALF * XP, ncol), lambda b: (0, 0)),
+        out_specs=pl.BlockSpec((ncol // 12, XP, 128), lambda b: (0, 0, 0)),
         scratch_shapes=[
             pltpu.VMEM((XP * slots, points), jnp.float32),
             pltpu.VMEM((slots * XP, points), jnp.bfloat16),
             pltpu.VMEM((HALF * 128, points), jnp.bfloat16),
             pltpu.VMEM((slots, 128), jnp.int32),
             pltpu.VMEM((2 * HALF * XP, ncol), jnp.float32),
+            pltpu.VMEM((ncol, 128), jnp.float32),
         ],
         compiler_params=pltpu.CompilerParams(
             dimension_semantics=("arbitrary",), vmem_limit_bytes=48 * 1024 * 1024
@@ -99,20 +107,173 @@
     )(ids, orbitals, potential.reshape(count, 1, points), batch_pairs)
 
 
-def phase_sum(blocks, info, cell_table, kpoints, first_atom, atoms):
-    cells = jnp.take(cell_table, info[2], axis=0).astype(jnp.float32)
-    angle = two_pi * jnp.dot(kpoints, cells.T, precision=lax.Precision.HIGHEST)
-    phases = jnp.stack([jnp.cos(angle), jnp.sin(angle)], axis=1)
-    row_hot = (
-        info[0][:, None] - first_atom == jnp.arange(ATOM_DEV, dtype=jnp.int32)[None, :]
-    ).astype(jnp.float32)
-    col_hot = (info[1][:, None] == jnp.arange(atoms, dtype=jnp.int32)[None, :]).astype(jnp.float32)
-    shaped = blocks.reshape(NAO, NAO, -1)
-    weighted = jnp.einsum(
-        "ksp,abp,pi->ksiabp", phases, shaped, row_hot, precision=lax.Precision.HIGHEST
+def exchange_kernel(
+    grid_count, kpt_count, send_ref, info_ref, cells_ref, kpt_ref, out_ref,
+    landed, shared, turned, flipped, hot, phase, send1, recv1, send2, recv2,
+):
+    g = lax.axis_index("grid")
+    k = lax.axis_index("kpt")
+    barrier = pltpu.get_barrier_semaphore()
+
+    def grid_peer(d):
+        return (lax.rem(g + d, grid_count), k)
+
+    def kpt_peer(d):
+        return (g, lax.rem(k + d, kpt_count))
+
+    for d in range(1, grid_count):
+        pl.semaphore_signal(barrier, inc=1, device_id=grid_peer(d), device_id_type=MESH)
+    for d in range(1, kpt_count):
+        pl.semaphore_signal(barrier, inc=1, device_id=kpt_peer(d), device_id_type=MESH)
+    pl.semaphore_wait(barrier, grid_count + kpt_count - 2)
+
+    outgoing = []
+    for d in range(1, grid_count):
+        peer = grid_peer(d)
+        copy = pltpu.make_async_remote_copy(
+            src_ref=send_ref.at[peer[0]],
+            dst_ref=landed.at[pl.ds(pl.multiple_of(g * XP, XP), XP), :],
+            send_sem=send1.at[d],
+            recv_sem=recv1.at[d],
+            device_id=peer,
+            device_id_type=MESH,
+        )
+        copy.start()
+        outgoing.append(copy)
+    landed[pl.ds(pl.multiple_of(g * XP, XP), XP), :] = send_ref[g]
+
+    pairs = grid_count * kpt_count
+    lanes = NAO * pairs
+    atoms = ATOM_DEV * grid_count
+    total = info_ref.shape[1]
+    pair = lax.broadcasted_iota(jnp.int32, (total, pairs), 1)
+    source = ((pair % grid_count) * kpt_count + pair // grid_count) * grid_count + g
+    pick = (lax.broadcasted_iota(jnp.int32, (total, pairs), 0) == source).astype(jnp.float32)
+    info = jnp.dot(
+        info_ref[...].astype(jnp.float32).astype(jnp.bfloat16),
+        pick.astype(jnp.bfloat16),
+        preferred_element_type=jnp.float32,
     )
-    dense = jnp.einsum("ksiabp,pj->ksiajb", weighted, col_hot, precision=lax.Precision.HIGHEST)
-    return dense.reshape(kpoints.shape[0], 2, ATOM_DEV, NAO, atoms * NAO)
+    lane = lax.broadcasted_iota(jnp.int32, (pairs, lanes), 1)
+    spread = (lane % pairs == lax.broadcasted_iota(jnp.int32, (pairs, lanes), 0)).astype(jnp.float32)
+    info = jnp.dot(
+        info.astype(jnp.bfloat16), spread.astype(jnp.bfloat16), preferred_element_type=jnp.float32
+    ).astype(jnp.int32)
+    first, second, cell = info[0:1], info[1:2], info[2:3]
+    angle = two_pi * jnp.sum(cells_ref[...].astype(jnp.float32) * kpt_ref[...], axis=1, keepdims=True)
+    at_cell = lax.broadcasted_iota(jnp.int32, (cells_ref.shape[0], lanes), 0) == cell
+    for part, values in enumerate((jnp.cos(angle), jnp.sin(angle))):
+        row = jnp.sum(jnp.where(at_cell, values, 0.0), axis=0, keepdims=True)
+        for i in range(ATOM_DEV):
+            at = part * ATOM_DEV + i
+            phase[at : at + 1, :] = jnp.where(first == g * ATOM_DEV + i, row, 0.0)
+    chunk = XP * NAO
+    for top in range(0, atoms * NAO, chunk):
+        row = lax.broadcasted_iota(jnp.int32, (chunk, lanes), 0)
+        atom = (row * 20165) // 262144
+        orbital = row - atom * NAO
+        match = lax.broadcasted_iota(jnp.int32, (chunk, lanes), 1) // pairs == orbital
+        match = match & (atom + top // NAO == second)
+        hot[top : top + chunk, :] = match.astype(jnp.float32).astype(jnp.bfloat16)
+
+    for copy in outgoing:
+        copy.wait()
+    half = grid_count // 2
+    for kind in range(2):
+        for par in range(2):
+            value = None
+            for s in range(3):
+                part = landed[pl.ds(kind * 6 + s * 2 + par, grid_count, stride=XP), :]
+                turn = (s - 1 + kind * half) % grid_count
+                if turn:
+                    part = pltpu.roll(part, turn, 0)
+                value = part if value is None else value + part
+            base = (kind * 2 + par) * grid_count
+            shared[k, base : base + grid_count, :] = value
+
+    outgoing = []
+    for d in range(1, kpt_count):
+        copy = pltpu.make_async_remote_copy(
+            src_ref=shared.at[k],
+            dst_ref=shared.at[k],
+            send_sem=send2.at[d],
+            recv_sem=recv2.at[d],
+            device_id=kpt_peer(d),
+            device_id_type=MESH,
+        )
+        copy.start()
+        outgoing.append(copy)
+    for copy in outgoing:
+        copy.wait()
+
+    width = min(2 * pairs, 128)
+    chunks = 2 * pairs // width
+    for kp in range(2):
+        block = jnp.concatenate(
+            [shared[c, kp * 2 * grid_count + par * grid_count : kp * 2 * grid_count + (par + 1) * grid_count, :]
+             for par in range(2) for c in range(kpt_count)],
+            axis=0,
+        )
+        block = jnp.transpose(block)
+        for t in range(chunks):
+            turned[kp * chunks + t] = block[:, t * width : (t + 1) * width]
+
+    def half_lanes(kind, par, rows):
+        if pairs < width:
+            return turned[kind, rows, :][:, par * pairs : (par + 1) * pairs]
+        parts = range(par * pairs // width, (par + 1) * pairs // width)
+        return jnp.concatenate([turned[kind * chunks + t, rows, :] for t in parts], axis=1)
+
+    flipped[...] = jnp.zeros_like(flipped)
+    for x in range(NAO):
+        for par in range(2):
+            flipped[par * HALF : (par + 1) * HALF, x * pairs : (x + 1) * pairs] = half_lanes(
+                1, par, pl.ds(x, HALF, stride=XP)
+            )
+    direct = jnp.concatenate(
+        [half_lanes(0, y // HALF, pl.ds((y % HALF) * XP, XP)) for y in range(NAO)], axis=1
+    )
+    sym = 0.5 * (direct + flipped[...])
+    rows = jnp.concatenate([sym * phase[at : at + 1, :] for at in range(2 * ATOM_DEV)], axis=0)
+    high = rows.astype(jnp.bfloat16)
+    low = (rows - high.astype(jnp.float32)).astype(jnp.bfloat16)
+    dense = lax.dot_general(
+        jnp.concatenate([high, low], axis=0), hot[...], NT, preferred_element_type=jnp.float32
+    )
+    count = 2 * ATOM_DEV * XP
+    dense = dense[:count] + dense[count:]
+    for at in range(2 * ATOM_DEV):
+        out_ref[0, at // ATOM_DEV, at % ATOM_DEV] = dense[at * XP : at * XP + NAO, :]
+
+
+def exchange(send, pair_info, cell_table, kpoints, grid_count, kpt_count):
+    pairs = grid_count * kpt_count
+    lanes = NAO * pairs
+    atoms = ATOM_DEV * grid_count
+    width = min(2 * pairs, 128)
+    chunks = 2 * pairs // width
+    vmem = pl.BlockSpec(memory_space=pltpu.VMEM)
+    return pl.pallas_call(
+        functools.partial(exchange_kernel, grid_count, kpt_count),
+        out_shape=jax.ShapeDtypeStruct((1, 2, ATOM_DEV, NAO, atoms * NAO), jnp.float32),
+        in_specs=[vmem] * 4,
+        out_specs=vmem,
+        scratch_shapes=[
+            pltpu.VMEM((grid_count * XP, 128), jnp.float32),
+            pltpu.VMEM((kpt_count, 4 * grid_count, 128), jnp.float32),
+            pltpu.VMEM((2 * chunks, 128, width), jnp.float32),
+            pltpu.VMEM((XP, lanes), jnp.float32),
+            pltpu.VMEM((atoms * NAO, lanes), jnp.bfloat16),
+            pltpu.VMEM((2 * ATOM_DEV, lanes), jnp.float32),
+            pltpu.SemaphoreType.DMA((grid_count,)),
+            pltpu.SemaphoreType.DMA((grid_count,)),
+            pltpu.SemaphoreType.DMA((kpt_count,)),
+            pltpu.SemaphoreType.DMA((kpt_count,)),
+        ],
+        compiler_params=pltpu.CompilerParams(
+            collective_id=0, has_side_effects=True, vmem_limit_bytes=56 * 1024 * 1024
+        ),
+    )(send, pair_info, cell_table, kpoints)
 
 
 def on_device(orbitals, potential, batch_pairs, pair_info, mirror, cell_table, kpoints):
@@ -120,7 +281,7 @@
     kpt_count = lax.axis_size("kpt")
     npairs = pair_info.shape[1]
     pair_dev = npairs // (grid_count * kpt_count)
-    row_pairs = pair_dev // grid_count
+    assert pair_dev == grid_count
     grid_pos = lax.axis_index("grid")
     kpt_pos = lax.axis_index("kpt")
     half = grid_count // 2
@@ -135,25 +296,8 @@
     ids = jnp.stack([pair_id(0), jnp.take(mirror, pair_id(half))])
     ids = ids[:, :, None, :] * 2 + jnp.arange(2, dtype=jnp.int32)[None, None, :, None]
     ids = jnp.broadcast_to(ids.reshape(-1, 1), (12 * pair_dev, 128))
-    table = integrate(ids, orbitals, potential, batch_pairs)
-    table = table.reshape(HALF, XP, 2, 3, 2, grid_count, row_pairs)[:, :NAO]
-    send = table.transpose(5, 2, 3, 6, 4, 0, 1)
-    got = lax.all_to_all(send, "grid", split_axis=0, concat_axis=0, tiled=True)
-    direct = sum(jnp.roll(got[:, 0, s], s - 1, axis=0) for s in range(3))
-    mirrored = sum(jnp.roll(got[:, 1, s], s - 1 + half, axis=0) for s in range(3))
-
-    def square(value):
-        return value.reshape(grid_count, row_pairs, 2 * HALF, NAO)[:, :, :NAO]
-
-    sym = 0.5 * (square(direct).transpose(3, 2, 0, 1) + square(mirrored).transpose(2, 3, 0, 1))
-    gathered = lax.all_gather(sym.reshape(NAO * NAO, 1, -1), "kpt", axis=1, tiled=True)
-    info = pair_info.reshape(3, grid_count, kpt_count, grid_count, row_pairs)
-    info = lax.dynamic_slice_in_dim(info, grid_pos, 1, 3)[:, :, :, 0]
-    info = info.transpose(0, 2, 1, 3).reshape(3, -1)
-    atoms = ATOM_DEV * grid_count
-    return phase_sum(
-        gathered.reshape(NAO * NAO, -1), info, cell_table, kpoints, grid_pos * ATOM_DEV, atoms
-    )
+    send = integrate(ids, orbitals, potential, batch_pairs)
+    return exchange(send, pair_info, cell_table, kpoints, grid_count, kpt_count)
 
 
 def solution(mesh):

time: 44.9 us -> 34.9 us (0.78)
  Pallas kernels: 15.7 us -> 29.8 us
  starting transfers between devices: 7.25 us -> 0 us
  blocking collectives: 5.19 us -> 0 us
  waiting for transfers between devices: 4.97 us -> 0 us
  local copies, waits for them, and re-layouts: 9.18 us -> 4.55 us
  other arithmetic: 1.12 us -> 0.26 us
  matrix products: 0.83 us -> 0 us
    pallas_call x0 -> x1, Pallas kernels: none -> 14.1 us  [exchange(): pl.pallas_call(functools.partial(exchange_kernel, grid_count, kpt_count),...]
    all_to_all x1 -> x0, starting transfers between devices: 7.25 us -> none  [on_device(): got = lax.all_to_all(send, 'grid', split_axis=0, concat_axis=0, tiled=True)]
    all_gather x1 -> x0, blocking collectives: 5.19 us -> none  [on_device(): lax.all_gather(sym.reshape(NAO * NAO, 1, -1), 'kpt', axis=1, tiled=True)]
    all_to_all x1 -> x0, waiting for transfers between devices: 4.97 us -> none  [on_device(): got = lax.all_to_all(send, 'grid', split_axis=0, concat_axis=0, tiled=True)]
    reshape x4 -> x0, local copies, waits for them, and re-layouts: 2.27 us -> none  [the longest x1 1.93 us: phase_sum(): return dense.reshape(kpoints.shape[0], 2, ATOM_DEV, NAO, atoms * NAO)]
    pallas_call x1, local copies, waits for them, and re-layouts: 0.08 us -> 1.77 us  [exchange(): pl.pallas_call(functools.partial(exchange_kernel, grid_count, kpt_count),...]
    transpose x3 -> x0, local copies, waits for them, and re-layouts: 0.98 us -> none  [the longest x1 0.68 us: phase_sum(): jnp.einsum('ksiabp,pj->ksiajb', weighted, col_hot, precision=lax.Precisio...]
    dot_general x2 -> x0, matrix products: 0.83 us -> none  [the longest x1 0.57 us: phase_sum(): jnp.einsum('ksiabp,pj->ksiajb', weighted, col_hot, precision=lax.Precisio...]
  transfers between devices with their start and end apart: 1 -> 0, of which waited for: 1 -> 0; matrix products, arithmetic and copies ran while one was open for 4% -> 0% of each run, Pallas kernels for 0% -> 0%
where the time goes in v2:
time: 34.9 us; the launch traced here: 34.7 us
  Pallas kernels  29.8 us (85%)
  local copies, waits for them, and re-layouts  4.55 us (13%)
    pallas_call x1, Pallas kernels, integrate(): pl.pallas_call(integrate_kernel, grid=(count,), out_shape=jax.ShapeDtypeS...  15.8 us
    pallas_call x1, Pallas kernels, exchange(): pl.pallas_call(functools.partial(exchange_kernel, grid_count, kpt_count),...  14.1 us
    pallas_call x1, local copies, waits for them, and re-layouts, exchange(): pl.pallas_call(functools.partial(exchange_kernel, grid_count, kpt_count),...  1.77 us
    unnamed x13, local copies, waits for them, and re-layouts  1.74 us
    gather x2, local copies, waits for them, and re-layouts, on_device(): ids = jnp.stack([pair_id(0), jnp.take(mirror, pair_id(half))])  0.79 us

profile of v2, /device:TPU:0, one launch (start us, length us, event | category | flops | bytes accessed | tf_op | source)
XLA Modules:
  0.0 34.7 jit_solution(8703587998195627699)
XLA Ops:
  0.0 0.0 copy-start
  0.0 0.0 copy-start.5
  0.0 0.0 copy-start.3
  0.0 0.0 copy-start.4
  0.0 0.0 copy-start.1
  0.0 0.1 iota_add_fusion.1
  0.1 0.1 compare_select_fusion
  0.2 0.1 reshape.226
  0.3 0.4 %copy-done = s32[256]{0:T(256)S(1)} copy-done((s32[256]{0:T(256)S(1)}, s32[256]{0:T(256)}, u32[]{:S(2)}) %copy-start) | copy-done | bytes 1048
  0.7 0.7 %gather_fusion = s32[24]{0:T(128)S(1)} fusion(s32[256]{0:T(256)S(1)} %copy-done, s32[1024]{0:T(1024)S(1)} %pad_clamp_fusion), kind=kCustom, calls=%fused_computation | custom fusion | bytes 288 | tf_op jit(solution)/shard_map/jit(_take)/gather | solution.py:296
  1.4 0.1 gather.7
  1.5 0.1 fusion.3
  1.6 0.1 add.215
  1.7 0.0 copy-done.5
  1.7 0.7 %copy.10.cells_ref = s32[61,3]{1,0:T(8,128)} copy(s32[61,3]{0,1:T(4,128)S(1)} %copy-done.5) | data formatting | bytes 1464 | tf_op args[5]
  2.4 0.1 broadcast_in_dim.4.ids_ref
  2.5 0.0 copy-done.3
  2.5 0.0 copy-done.4
  2.5 0.0 copy-done.1
  2.5 15.8 %shard_map.73.send_ref = f32[8,16,128]{2,1,0:T(8,128)S(1)} custom-call(s32[96,128]{1,0:T(8,128)S(1)} %broadcast_in_dim.4.ids_ref, bf16[8,13,48,128]{3,2,1,0:T(8,128)(2,1)S(1)} %copy-done.1, f32[8,1,128]{2,1,0:T(1,128)S(1)} %bitcast.3, s32[8,48,48]{2,1,0:T(8,128)S(1)} %copy-done.3), custom_call_target="tpu_custom_call" | custom-call | tf_op jit(solution)/shard_map/pallas_call | solution.py:85
  18.2 0.0 copy-start.2
  18.3 0.6 %copy-done.2 = f32[8,16,128]{2,1,0:T(8,128)} copy-done((f32[8,16,128]{2,1,0:T(8,128)}, f32[8,16,128]{2,1,0:T(8,128)S(1)}, u32[]{:S(2)}) %copy-start.2) | copy-done | bytes 65560
  18.9 14.1 %shard_map.74 = f32[1,2,4,13,416]{4,3,2,1,0:T(8,128)} custom-call(f32[8,16,128]{2,1,0:T(8,128)} %copy-done.2, s32[3,256]{1,0:T(4,128)} %info_ref.1, s32[61,3]{1,0:T(8,128)} %copy.10.cells_ref, f32[1,3]{1,0:T(1,128)} %kpt_ref.1), custom_call_target="tpu_custom_call" | custom-call | tf_op jit(solution)/shard_map/pallas_call | solution.py:256
  32.9 1.8 %copy.11 = f32[1,2,4,13,416]{4,2,3,1,0:T(4,128)} copy(f32[1,2,4,13,416]{4,3,2,1,0:T(8,128)} %shard_map.74) | data formatting | bytes 346112 | tf_op jit(solution)/shard_map/pallas_call | solution.py:256
  (4 shorter events, 0.0 us)
Async XLA Ops:
  0.0 0.7 %copy-start = (s32[256]{0:T(256)S(1)}, s32[256]{0:T(256)}, u32[]{:S(2)}) copy-start(s32[256]{0:T(256)} %param.11) | copy-start | bytes 3076
  0.0 1.7 %copy-start.5 = (s32[61,3]{0,1:T(4,128)S(1)}, s32[61,3]{0,1:T(4,128)}, u32[]{:S(2)}) copy-start(s32[61,3]{0,1:T(4,128)} %param.12) | copy-start | bytes 2200
  0.0 2.4 %copy-start.3 = (s32[8,48,48]{2,1,0:T(8,128)S(1)}, s32[8,48,48]{2,1,0:T(8,128)}, u32[]{:S(2)}) copy-start(s32[8,48,48]{2,1,0:T(8,128)} %pairs_ref.1) | copy-start | bytes 221188
  0.0 2.4 %copy-start.4 = (f32[8,128]{1,0:T(8,128)S(1)}, f32[8,128]{1,0:T(8,128)}, u32[]{:S(2)}) copy-start(f32[8,128]{1,0:T(8,128)} %param.8) | copy-start | bytes 12292
  0.0 2.5 %copy-start.1 = (bf16[8,13,48,128]{3,2,1,0:T(8,128)(2,1)S(1)}, bf16[8,13,48,128]{3,2,1,0:T(8,128)(2,1)}, u32[]{:S(2)}) copy-start(bf16[8,13,48,128]{3,2,1,0:T(8,128)(2,1)} %orb_ref.1) | copy-start | bytes 3833860
  18.2 0.6 %copy-start.2 = (f32[8,16,128]{2,1,0:T(8,128)}, f32[8,16,128]{2,1,0:T(8,128)S(1)}, u32[]{:S(2)}) copy-start(f32[8,16,128]{2,1,0:T(8,128)S(1)} %shard_map.73.send_ref) | copy-start | bytes 196612

commit v3 on v2

--- a/solution.py
+++ b/solution.py
@@ -21,10 +21,17 @@
 
 
 def integrate_kernel(
-    ids_ref, orb_ref, pot_ref, pairs_ref, out_ref, rows_f32, left, right, codes, acc, turned
+    grid_count, kpt_count, orb_ref, pot_ref, pairs_ref, mirror_ref, out_ref,
+    rows_f32, left, right, codes, ids, acc, turned,
 ):
     step = pl.program_id(0)
     _, width, slots, points = orb_ref.shape
+    pair_dev = out_ref.shape[0]
+    g = lax.axis_index("grid")
+    k = lax.axis_index("kpt")
+
+    def first_pair(offset):
+        return (lax.rem(g + offset + grid_count, grid_count) * kpt_count + k) * pair_dev
 
     @pl.when(step == 0)
     def _():
@@ -32,6 +39,11 @@
         right[...] = jnp.zeros_like(right)
         codes[...] = jnp.full_like(codes, -1)
         acc[...] = jnp.zeros_like(acc)
+        slot = lax.broadcasted_iota(jnp.int32, (pair_dev, 128), 0)
+        for s in range(3):
+            for par in range(2):
+                at = (s * 2 + par) * pair_dev
+                ids[at : at + pair_dev, :] = (slot + first_pair(s - 1)) * 2 + par
 
     weight = pot_ref[0]
     for y in range(width):
@@ -44,7 +56,7 @@
     pairs = pairs_ref[0]
     codes[:, 0:slots] = pairs * 2
     codes[:, CP : CP + slots] = pairs * 2 + 1
-    ids = ids_ref[...]
+    wanted = ids[...]
     for a0 in range(0, slots, A_STEP):
         prod = lax.dot_general(
             left[a0 * XP : (a0 + A_STEP) * XP, :], right[...], NT, preferred_element_type=jnp.float32
@@ -60,11 +72,11 @@
             ]
             cols.append(jnp.concatenate(parts, axis=0))
             hots.append(
-                (codes[a0 + a : a0 + a + 1, :] == ids).astype(jnp.float32).astype(jnp.bfloat16)
+                (codes[a0 + a : a0 + a + 1, :] == wanted).astype(jnp.float32).astype(jnp.bfloat16)
             )
         acc[...] += lax.dot_general(
+            jnp.concatenate(hots, axis=1),
             jnp.concatenate(cols, axis=1),
-            jnp.concatenate(hots, axis=1),
             NT,
             preferred_element_type=jnp.float32,
         )
@@ -73,38 +85,56 @@
     def _():
         half = HALF * XP
         out_ref[...] = jnp.zeros_like(out_ref)
-        turned[:, 0:half] = jnp.transpose(acc[:half, :] + acc[half:, :])
-        pair_dev = out_ref.shape[0]
+        table = acc[:, :half] + acc[:, half:]
+        count = 6 * pair_dev
+        turned[0:count, 0:half] = table
+        npairs = mirror_ref.shape[1]
+        every = lax.broadcasted_iota(jnp.int32, (pair_dev, npairs), 1)
+        row = lax.broadcasted_iota(jnp.int32, (pair_dev, npairs), 0)
+        partner = mirror_ref[...].astype(jnp.float32)
+        col = lax.broadcasted_iota(jnp.int32, (pair_dev, pair_dev), 1)
+        for s in range(3):
+            at_pair = every == row + first_pair(s - 1 + grid_count // 2)
+            source = jnp.sum(jnp.where(at_pair, partner, 0.0), axis=1, keepdims=True)
+            swap = (source == (col + first_pair(s - 1)).astype(jnp.float32)).astype(jnp.float32)
+            for par in range(2):
+                at = (s * 2 + par) * pair_dev
+                turned[count + at : count + at + pair_dev, 0:half] = jnp.dot(
+                    swap,
+                    table[at : at + pair_dev, :],
+                    precision=lax.Precision.HIGHEST,
+                    preferred_element_type=jnp.float32,
+                )
         for q in range(pair_dev):
             out_ref[q, 0:12, 0:half] = turned[pl.ds(q, 12, stride=pair_dev), 0:half]
 
 
-def integrate(ids, orbitals, potential, batch_pairs):
+def integrate(orbitals, potential, batch_pairs, mirror, grid_count, kpt_count, pair_dev):
     count, width, slots, points = orbitals.shape
-    ncol = ids.shape[0]
     return pl.pallas_call(
-        integrate_kernel,
+        functools.partial(integrate_kernel, grid_count, kpt_count),
         grid=(count,),
-        out_shape=jax.ShapeDtypeStruct((ncol // 12, XP, 128), jnp.float32),
+        out_shape=jax.ShapeDtypeStruct((pair_dev, XP, 128), jnp.float32),
         in_specs=[
-            pl.BlockSpec((ncol, 128), lambda b: (0, 0)),
             pl.BlockSpec((1, width, slots, points), lambda b: (b, 0, 0, 0)),
             pl.BlockSpec((1, 1, points), lambda b: (b, 0, 0)),
             pl.BlockSpec((1, slots, slots), lambda b: (b, 0, 0)),
+            pl.BlockSpec((1, mirror.shape[0]), lambda b: (0, 0)),
         ],
-        out_specs=pl.BlockSpec((ncol // 12, XP, 128), lambda b: (0, 0, 0)),
+        out_specs=pl.BlockSpec((pair_dev, XP, 128), lambda b: (0, 0, 0)),
         scratch_shapes=[
             pltpu.VMEM((XP * slots, points), jnp.float32),
             pltpu.VMEM((slots * XP, points), jnp.bfloat16),
             pltpu.VMEM((HALF * 128, points), jnp.bfloat16),
             pltpu.VMEM((slots, 128), jnp.int32),
-            pltpu.VMEM((2 * HALF * XP, ncol), jnp.float32),
-            pltpu.VMEM((ncol, 128), jnp.float32),
+            pltpu.VMEM((6 * pair_dev, 128), jnp.int32),
+            pltpu.VMEM((6 * pair_dev, 2 * HALF * XP), jnp.float32),
+            pltpu.VMEM((12 * pair_dev, 128), jnp.float32),
         ],
         compiler_params=pltpu.CompilerParams(
             dimension_semantics=("arbitrary",), vmem_limit_bytes=48 * 1024 * 1024
         ),
-    )(ids, orbitals, potential.reshape(count, 1, points), batch_pairs)
+    )(orbitals, potential.reshape(count, 1, points), batch_pairs, mirror.reshape(1, -1))
 
 
 def exchange_kernel(
@@ -125,6 +155,45 @@
         pl.semaphore_signal(barrier, inc=1, device_id=grid_peer(d), device_id_type=MESH)
     for d in range(1, kpt_count):
         pl.semaphore_signal(barrier, inc=1, device_id=kpt_peer(d), device_id_type=MESH)
+    pairs = grid_count * kpt_count
+    lanes = NAO * pairs
+    atoms = ATOM_DEV * grid_count
+    total = info_ref.shape[1]
+    pair = lax.broadcasted_iota(jnp.int32, (1, pairs), 1)
+    source = ((pair % grid_count) * kpt_count + pair // grid_count) * grid_count + g
+    pick = (lax.broadcasted_iota(jnp.int32, (total, pairs), 0) == source).astype(jnp.float32)
+    info = jnp.dot(
+        info_ref[...].astype(jnp.float32).astype(jnp.bfloat16),
+        pick.astype(jnp.bfloat16),
+        preferred_element_type=jnp.float32,
+    )
+    lane = lax.broadcasted_iota(jnp.int32, (1, lanes), 1)
+    lane_orbital = lane // pairs
+    lane_pair = lane - lane_orbital * pairs
+    spread = (lane_pair == lax.broadcasted_iota(jnp.int32, (pairs, lanes), 0)).astype(jnp.float32)
+    info = jnp.dot(
+        info.astype(jnp.bfloat16), spread.astype(jnp.bfloat16), preferred_element_type=jnp.float32
+    ).astype(jnp.int32)
+    first, second, cell = info[0:1], info[1:2], info[2:3]
+    vectors = cells_ref[...].astype(jnp.float32)
+    angle = vectors[0:1] * kpt_ref[0, 0]
+    for d in range(1, 3):
+        angle = angle + vectors[d : d + 1] * kpt_ref[0, d]
+    angle = two_pi * angle
+    at_cell = lax.broadcasted_iota(jnp.int32, (cells_ref.shape[1], lanes), 0) == cell
+    values = jnp.dot(
+        jnp.concatenate([jnp.cos(angle), jnp.sin(angle)], axis=0),
+        at_cell.astype(jnp.float32),
+        precision=lax.Precision.HIGHEST,
+        preferred_element_type=jnp.float32,
+    )
+    for part in range(2):
+        for i in range(ATOM_DEV):
+            at = part * ATOM_DEV + i
+            phase[at : at + 1, :] = jnp.where(
+                first == g * ATOM_DEV + i, values[part : part + 1], 0.0
+            )
+
     pl.semaphore_wait(barrier, grid_count + kpt_count - 2)
 
     outgoing = []
@@ -142,39 +211,11 @@
         outgoing.append(copy)
     landed[pl.ds(pl.multiple_of(g * XP, XP), XP), :] = send_ref[g]
 
-    pairs = grid_count * kpt_count
-    lanes = NAO * pairs
-    atoms = ATOM_DEV * grid_count
-    total = info_ref.shape[1]
-    pair = lax.broadcasted_iota(jnp.int32, (total, pairs), 1)
-    source = ((pair % grid_count) * kpt_count + pair // grid_count) * grid_count + g
-    pick = (lax.broadcasted_iota(jnp.int32, (total, pairs), 0) == source).astype(jnp.float32)
-    info = jnp.dot(
-        info_ref[...].astype(jnp.float32).astype(jnp.bfloat16),
-        pick.astype(jnp.bfloat16),
-        preferred_element_type=jnp.float32,
-    )
-    lane = lax.broadcasted_iota(jnp.int32, (pairs, lanes), 1)
-    spread = (lane % pairs == lax.broadcasted_iota(jnp.int32, (pairs, lanes), 0)).astype(jnp.float32)
-    info = jnp.dot(
-        info.astype(jnp.bfloat16), spread.astype(jnp.bfloat16), preferred_element_type=jnp.float32
-    ).astype(jnp.int32)
-    first, second, cell = info[0:1], info[1:2], info[2:3]
-    angle = two_pi * jnp.sum(cells_ref[...].astype(jnp.float32) * kpt_ref[...], axis=1, keepdims=True)
-    at_cell = lax.broadcasted_iota(jnp.int32, (cells_ref.shape[0], lanes), 0) == cell
-    for part, values in enumerate((jnp.cos(angle), jnp.sin(angle))):
-        row = jnp.sum(jnp.where(at_cell, values, 0.0), axis=0, keepdims=True)
-        for i in range(ATOM_DEV):
-            at = part * ATOM_DEV + i
-            phase[at : at + 1, :] = jnp.where(first == g * ATOM_DEV + i, row, 0.0)
     chunk = XP * NAO
+    target = second * NAO + lane_orbital
+    row = lax.broadcasted_iota(jnp.int32, (chunk, lanes), 0)
     for top in range(0, atoms * NAO, chunk):
-        row = lax.broadcasted_iota(jnp.int32, (chunk, lanes), 0)
-        atom = (row * 20165) // 262144
-        orbital = row - atom * NAO
-        match = lax.broadcasted_iota(jnp.int32, (chunk, lanes), 1) // pairs == orbital
-        match = match & (atom + top // NAO == second)
-        hot[top : top + chunk, :] = match.astype(jnp.float32).astype(jnp.bfloat16)
+        hot[top : top + chunk, :] = (row == target - top).astype(jnp.float32).astype(jnp.bfloat16)
 
     for copy in outgoing:
         copy.wait()
@@ -256,7 +297,7 @@
     return pl.pallas_call(
         functools.partial(exchange_kernel, grid_count, kpt_count),
         out_shape=jax.ShapeDtypeStruct((1, 2, ATOM_DEV, NAO, atoms * NAO), jnp.float32),
-        in_specs=[vmem] * 4,
+        in_specs=[vmem, vmem, vmem, pl.BlockSpec(memory_space=pltpu.SMEM)],
         out_specs=vmem,
         scratch_shapes=[
             pltpu.VMEM((grid_count * XP, 128), jnp.float32),
@@ -273,7 +314,7 @@
         compiler_params=pltpu.CompilerParams(
             collective_id=0, has_side_effects=True, vmem_limit_bytes=56 * 1024 * 1024
         ),
-    )(send, pair_info, cell_table, kpoints)
+    )(send, pair_info, cell_table.T, kpoints)
 
 
 def on_device(orbitals, potential, batch_pairs, pair_info, mirror, cell_table, kpoints):
@@ -282,21 +323,7 @@
     npairs = pair_info.shape[1]
     pair_dev = npairs // (grid_count * kpt_count)
     assert pair_dev == grid_count
-    grid_pos = lax.axis_index("grid")
-    kpt_pos = lax.axis_index("kpt")
-    half = grid_count // 2
-
-    shift = jnp.arange(-1, 2, dtype=jnp.int32)[:, None]
-    slot = jnp.arange(pair_dev, dtype=jnp.int32)[None, :]
-
-    def pair_id(offset):
-        holder = (grid_pos + shift + offset + grid_count) % grid_count
-        return (holder * kpt_count + kpt_pos) * pair_dev + slot
-
-    ids = jnp.stack([pair_id(0), jnp.take(mirror, pair_id(half))])
-    ids = ids[:, :, None, :] * 2 + jnp.arange(2, dtype=jnp.int32)[None, None, :, None]
-    ids = jnp.broadcast_to(ids.reshape(-1, 1), (12 * pair_dev, 128))
-    send = integrate(ids, orbitals, potential, batch_pairs)
+    send = integrate(orbitals, potential, batch_pairs, mirror, grid_count, kpt_count, pair_dev)
     return exchange(send, pair_info, cell_table, kpoints, grid_count, kpt_count)
 
 

time: 34.9 us -> 34.3 us (0.983)
  Pallas kernels: 29.8 us -> 28 us
  local copies, waits for them, and re-layouts: 4.55 us -> 6.02 us
    unnamed x13 -> x10, local copies, waits for them, and re-layouts: 1.74 us -> 4.24 us
    pallas_call x1, Pallas kernels: 15.8 us -> 13.9 us  [integrate(): pl.pallas_call(functools.partial(integrate_kernel, grid_count, kpt_count)...]
    gather x2 -> x0, local copies, waits for them, and re-layouts: 0.79 us -> none  [on_device(): ids = jnp.stack([pair_id(0), jnp.take(mirror, pair_id(half))])]
where the time goes in v3:
time: 34.3 us; the launch traced here: 34 us
  Pallas kernels  28 us (82%)
  local copies, waits for them, and re-layouts  6.02 us (18%)
    pallas_call x1, Pallas kernels, exchange(): pl.pallas_call(functools.partial(exchange_kernel, grid_count, kpt_count),...  14.1 us
    pallas_call x1, Pallas kernels, integrate(): pl.pallas_call(functools.partial(integrate_kernel, grid_count, kpt_count)...  13.9 us
    unnamed x10, local copies, waits for them, and re-layouts  4.24 us
    pallas_call x1, local copies, waits for them, and re-layouts, exchange(): pl.pallas_call(functools.partial(exchange_kernel, grid_count, kpt_count),...  1.77 us

profile of v3, /device:TPU:0, one launch (start us, length us, event | category | flops | bytes accessed | tf_op | source)
XLA Modules:
  0.0 34.0 jit_solution(7117792839516229695)
XLA Ops:
  0.0 0.0 copy-start
  0.0 1.3 %copy-done = bf16[8,13,48,128]{3,2,1,0:T(8,128)(2,1)S(1)} copy-done((bf16[8,13,48,128]{3,2,1,0:T(8,128)(2,1)S(1)}, bf16[8,13,48,128]{3,2,1,0:T(8,128)(2,1)}, u32[]{:S(2)}) %copy-start) | copy-done | bytes 1277976
  1.3 0.0 copy-start.2
  1.3 0.9 %copy-done.2 = s32[8,48,48]{2,1,0:T(8,128)S(1)} copy-done((s32[8,48,48]{2,1,0:T(8,128)S(1)}, s32[8,48,48]{2,1,0:T(8,128)}, u32[]{:S(2)}) %copy-start.2) | copy-done | bytes 73752
  2.2 0.0 copy-start.3
  2.2 0.7 %copy-done.3 = f32[8,128]{1,0:T(8,128)S(1)} copy-done((f32[8,128]{1,0:T(8,128)S(1)}, f32[8,128]{1,0:T(8,128)}, u32[]{:S(2)}) %copy-start.3) | copy-done | bytes 4120
  2.9 0.0 copy-start.4
  2.9 0.7 %copy-done.4 = s32[256]{0:T(256)S(1)} copy-done((s32[256]{0:T(256)S(1)}, s32[256]{0:T(256)}, u32[]{:S(2)}) %copy-start.4) | copy-done | bytes 1048
  3.6 13.9 %shard_map.73.send_ref = f32[8,16,128]{2,1,0:T(8,128)S(1)} custom-call(bf16[8,13,48,128]{3,2,1,0:T(8,128)(2,1)S(1)} %copy-done, f32[8,1,128]{2,1,0:T(1,128)S(1)} %bitcast.3, s32[8,48,48]{2,1,0:T(8,128)S(1)} %copy-done.2, s32[1,256]{1,0:T(1,128)S(1)} %bitcast.4), custom_call_target="tpu_custom_call" | custom-call | tf_op jit(solution)/shard_map/pallas_call | solution.py:114
  17.5 0.0 copy-start.1
  17.5 0.6 %copy-done.1 = f32[8,16,128]{2,1,0:T(8,128)} copy-done((f32[8,16,128]{2,1,0:T(8,128)}, f32[8,16,128]{2,1,0:T(8,128)S(1)}, u32[]{:S(2)}) %copy-start.1) | copy-done | bytes 65560
  18.1 14.1 %shard_map.74 = f32[1,2,4,13,416]{4,3,2,1,0:T(8,128)} custom-call(f32[8,16,128]{2,1,0:T(8,128)} %copy-done.1, s32[3,256]{1,0:T(4,128)} %info_ref.1, s32[3,61]{1,0:T(4,128)} %bitcast.5, f32[1,3]{1,0:T(1,128)} %kpt_ref.1), custom_call_target="tpu_custom_call" | custom-call | tf_op jit(solution)/shard_map/pallas_call | solution.py:297
  32.2 1.8 %copy.8 = f32[1,2,4,13,416]{4,2,3,1,0:T(4,128)} copy(f32[1,2,4,13,416]{4,3,2,1,0:T(8,128)} %shard_map.74) | data formatting | bytes 346112 | tf_op jit(solution)/shard_map/pallas_call | solution.py:297
Async XLA Ops:
  0.0 1.3 %copy-start = (bf16[8,13,48,128]{3,2,1,0:T(8,128)(2,1)S(1)}, bf16[8,13,48,128]{3,2,1,0:T(8,128)(2,1)}, u32[]{:S(2)}) copy-start(bf16[8,13,48,128]{3,2,1,0:T(8,128)(2,1)} %orb_ref.1) | copy-start | bytes 3833860
  1.3 0.9 %copy-start.2 = (s32[8,48,48]{2,1,0:T(8,128)S(1)}, s32[8,48,48]{2,1,0:T(8,128)}, u32[]{:S(2)}) copy-start(s32[8,48,48]{2,1,0:T(8,128)} %pairs_ref.1) | copy-start | bytes 221188
  2.2 0.7 %copy-start.3 = (f32[8,128]{1,0:T(8,128)S(1)}, f32[8,128]{1,0:T(8,128)}, u32[]{:S(2)}) copy-start(f32[8,128]{1,0:T(8,128)} %param.8) | copy-start | bytes 12292
  2.9 0.7 %copy-start.4 = (s32[256]{0:T(256)S(1)}, s32[256]{0:T(256)}, u32[]{:S(2)}) copy-start(s32[256]{0:T(256)} %param.11) | copy-start | bytes 3076
  17.5 0.6 %copy-start.1 = (f32[8,16,128]{2,1,0:T(8,128)}, f32[8,16,128]{2,1,0:T(8,128)S(1)}, u32[]{:S(2)}) copy-start(f32[8,16,128]{2,1,0:T(8,128)S(1)} %shard_map.73.send_ref) | copy-start | bytes 196612

commit v4 on v1

v4 whole, which is shorter than its diff:
```python
import functools
import math

import jax
import jax.numpy as jnp
from jax import lax
from jax.experimental import pallas as pl
from jax.experimental.pallas import tpu as pltpu
from jax.sharding import PartitionSpec as P

NAO = 13
XP = 16
HALF = 7
CP = 64
ATOM_DEV = 4
A_STEP = 8

two_pi = 2.0 * math.pi
MESH = pl.DeviceIdType.MESH
NT = (((1,), (1,)), ((), ()))


def whole_kernel(
    grid_count, kpt_count, orb_ref, pot_ref, pairs_ref, mirror_ref, info_ref, cells_ref, kpt_ref,
    out_ref, rows_f32, left, right, codes, ids, acc, table2, send,
    landed, shared, turned, flipped, hot, phase, send1, recv1, send2, recv2,
):
    step = pl.program_id(0)
    _, width, slots, points = orb_ref.shape
    pair_dev = send.shape[0]
    g = lax.axis_index("grid")
    k = lax.axis_index("kpt")

    def first_pair(offset):
        return (lax.rem(g + offset + grid_count, grid_count) * kpt_count + k) * pair_dev

    barrier = pltpu.get_barrier_semaphore()

    def grid_peer(d):
        return (lax.rem(g + d, grid_count), k)

    def kpt_peer(d):
        return (g, lax.rem(k + d, kpt_count))

    @pl.when(step == 0)
    def _():
        for d in range(1, grid_count):
            pl.semaphore_signal(barrier, inc=1, device_id=grid_peer(d), device_id_type=MESH)
        for d in range(1, kpt_count):
            pl.semaphore_signal(barrier, inc=1, device_id=kpt_peer(d), device_id_type=MESH)
        rows_f32[...] = jnp.zeros_like(rows_f32)
        right[...] = jnp.zeros_like(right)
        codes[...] = jnp.full_like(codes, -1)
        acc[...] = jnp.zeros_like(acc)
        slot = lax.broadcasted_iota(jnp.int32, (pair_dev, 128), 0)
        for s in range(3):
            for par in range(2):
                at = (s * 2 + par) * pair_dev
                ids[at : at + pair_dev, :] = (slot + first_pair(s - 1)) * 2 + par

    weight = pot_ref[0]
    for y in range(width):
        vals = orb_ref[0, y].astype(jnp.float32)
        base = (y % HALF) * 128 + (y // HALF) * CP
        right[base : base + slots, :] = (vals * weight).astype(jnp.bfloat16)
        rows_f32[y * slots : (y + 1) * slots, :] = vals
    for a in range(slots):
        left[a * XP : (a + 1) * XP, :] = rows_f32[pl.ds(a, XP, stride=slots), :].astype(jnp.bfloat16)
    pairs = pairs_ref[0]
    codes[:, 0:slots] = pairs * 2
    codes[:, CP : CP + slots] = pairs * 2 + 1
    wanted = ids[...]
    for a0 in range(0, slots, A_STEP):
        prod = lax.dot_general(
            left[a0 * XP : (a0 + A_STEP) * XP, :], right[...], NT, preferred_element_type=jnp.float32
        )
        high = prod.astype(jnp.bfloat16)
        low = (prod - high.astype(jnp.float32)).astype(jnp.bfloat16)
        cols, hots = [], []
        for a in range(A_STEP):
            parts = [
                part[a * XP : (a + 1) * XP, yp * 128 : (yp + 1) * 128]
                for part in (high, low)
                for yp in range(HALF)
            ]
            cols.append(jnp.concatenate(parts, axis=0))
            hots.append(
                (codes[a0 + a : a0 + a + 1, :] == wanted).astype(jnp.float32).astype(jnp.bfloat16)
            )
        acc[...] += lax.dot_general(
            jnp.concatenate(hots, axis=1),
            jnp.concatenate(cols, axis=1),
            NT,
            preferred_element_type=jnp.float32,
        )

    @pl.when(step == pl.num_programs(0) - 1)
    def _():
        half = HALF * XP
        send[...] = jnp.zeros_like(send)
        table = acc[:, :half] + acc[:, half:]
        count = 6 * pair_dev
        table2[0:count, 0:half] = table
        npairs = mirror_ref.shape[1]
        every = lax.broadcasted_iota(jnp.int32, (pair_dev, npairs), 1)
        row = lax.broadcasted_iota(jnp.int32, (pair_dev, npairs), 0)
        partner = mirror_ref[...].astype(jnp.float32)
        col = lax.broadcasted_iota(jnp.int32, (pair_dev, pair_dev), 1)
        for s in range(3):
            at_pair = every == row + first_pair(s - 1 + grid_count // 2)
            source = jnp.sum(jnp.where(at_pair, partner, 0.0), axis=1, keepdims=True)
            swap = (source == (col + first_pair(s - 1)).astype(jnp.float32)).astype(jnp.float32)
            for par in range(2):
                at = (s * 2 + par) * pair_dev
                table2[count + at : count + at + pair_dev, 0:half] = jnp.dot(
                    swap,
                    table[at : at + pair_dev, :],
                    precision=lax.Precision.HIGHEST,
                    preferred_element_type=jnp.float32,
                )
        for q in range(pair_dev):
            send[q, 0:12, 0:half] = table2[pl.ds(q, 12, stride=pair_dev), 0:half]
        pl.semaphore_wait(barrier, grid_count + kpt_count - 2)

        outgoing = []
        for d in range(1, grid_count):
            peer = grid_peer(d)
            copy = pltpu.make_async_remote_copy(
                src_ref=send.at[peer[0]],
                dst_ref=landed.at[pl.ds(pl.multiple_of(g * XP, XP), XP), :],
                send_sem=send1.at[d],
                recv_sem=recv1.at[d],
                device_id=peer,
                device_id_type=MESH,
            )
            copy.start()
            outgoing.append(copy)
        landed[pl.ds(pl.multiple_of(g * XP, XP), XP), :] = send[g]

        pairs = grid_count * kpt_count
        lanes = NAO * pairs
        atoms = ATOM_DEV * grid_count
        total = info_ref.shape[1]
        pair = lax.broadcasted_iota(jnp.int32, (1, pairs), 1)
        source = ((pair % grid_count) * kpt_count + pair // grid_count) * grid_count + g
        pick = (lax.broadcasted_iota(jnp.int32, (total, pairs), 0) == source).astype(jnp.float32)
        info = jnp.dot(
            info_ref[...].astype(jnp.float32).astype(jnp.bfloat16),
            pick.astype(jnp.bfloat16),
            preferred_element_type=jnp.float32,
        )
        lane = lax.broadcasted_iota(jnp.int32, (1, lanes), 1)
        lane_orbital = lane // pairs
        lane_pair = lane - lane_orbital * pairs
        spread = (lane_pair == lax.broadcasted_iota(jnp.int32, (pairs, lanes), 0)).astype(jnp.float32)
        info = jnp.dot(
            info.astype(jnp.bfloat16), spread.astype(jnp.bfloat16), preferred_element_type=jnp.float32
        ).astype(jnp.int32)
        first, second, cell = info[0:1], info[1:2], info[2:3]
        vectors = cells_ref[...].astype(jnp.float32)
        angle = vectors[0:1] * kpt_ref[0, 0]
        for d in range(1, 3):
            angle = angle + vectors[d : d + 1] * kpt_ref[0, d]
        angle = two_pi * angle
        at_cell = lax.broadcasted_iota(jnp.int32, (cells_ref.shape[1], lanes), 0) == cell
        values = jnp.dot(
            jnp.concatenate([jnp.cos(angle), jnp.sin(angle)], axis=0),
            at_cell.astype(jnp.float32),
            precision=lax.Precision.HIGHEST,
            preferred_element_type=jnp.float32,
        )
        for part in range(2):
            for i in range(ATOM_DEV):
                at = part * ATOM_DEV + i
                phase[at : at + 1, :] = jnp.where(
                    first == g * ATOM_DEV + i, values[part : part + 1], 0.0
                )

        chunk = XP * NAO
        target = second * NAO + lane_orbital
        row = lax.broadcasted_iota(jnp.int32, (chunk, lanes), 0)
        for top in range(0, atoms * NAO, chunk):
            hot[top : top + chunk, :] = (row == target - top).astype(jnp.float32).astype(jnp.bfloat16)

        for copy in outgoing:
            copy.wait()
        half = grid_count // 2
        for kind in range(2):
            for par in range(2):
                value = None
                for s in range(3):
                    part = landed[pl.ds(kind * 6 + s * 2 + par, grid_count, stride=XP), :]
                    turn = (s - 1 + kind * half) % grid_count
                    if turn:
                        part = pltpu.roll(part, turn, 0)
                    value = part if value is None else value + part
                base = (kind * 2 + par) * grid_count
                shared[k, base : base + grid_count, :] = value

        outgoing = []
        for d in range(1, kpt_count):
            copy = pltpu.make_async_remote_copy(
                src_ref=shared.at[k],
                dst_ref=shared.at[k],
                send_sem=send2.at[d],
                recv_sem=recv2.at[d],
                device_id=kpt_peer(d),
                device_id_type=MESH,
            )
            copy.start()
            outgoing.append(copy)
        for copy in outgoing:
            copy.wait()

        width = min(2 * pairs, 128)
        chunks = 2 * pairs // width
        for kp in range(2):
            block = jnp.concatenate(
                [shared[c, kp * 2 * grid_count + par * grid_count : kp * 2 * grid_count + (par + 1) * grid_count, :]
                 for par in range(2) for c in range(kpt_count)],
                axis=0,
            )
            block = jnp.transpose(block)
            for t in range(chunks):
                turned[kp * chunks + t] = block[:, t * width : (t + 1) * width]

        def half_lanes(kind, par, rows):
            if pairs < width:
                return turned[kind, rows, :][:, par * pairs : (par + 1) * pairs]
            parts = range(par * pairs // width, (par + 1) * pairs // width)
            return jnp.concatenate([turned[kind * chunks + t, rows, :] for t in parts], axis=1)

        flipped[...] = jnp.zeros_like(flipped)
        for x in range(NAO):
            for par in range(2):
                flipped[par * HALF : (par + 1) * HALF, x * pairs : (x + 1) * pairs] = half_lanes(
                    1, par, pl.ds(x, HALF, stride=XP)
                )
        direct = jnp.concatenate(
            [half_lanes(0, y // HALF, pl.ds((y % HALF) * XP, XP)) for y in range(NAO)], axis=1
        )
        sym = 0.5 * (direct + flipped[...])
        rows = jnp.concatenate([sym * phase[at : at + 1, :] for at in range(2 * ATOM_DEV)], axis=0)
        high = rows.astype(jnp.bfloat16)
        low = (rows - high.astype(jnp.float32)).astype(jnp.bfloat16)
        dense = lax.dot_general(
            jnp.concatenate([high, low], axis=0), hot[...], NT, preferred_element_type=jnp.float32
        )
        count = 2 * ATOM_DEV * XP
        dense = dense[:count] + dense[count:]
        for at in range(2 * ATOM_DEV):
            out_ref[0, at // ATOM_DEV, :, at % ATOM_DEV, :] = dense[at * XP : at * XP + NAO, :]


def whole(orbitals, potential, batch_pairs, mirror, pair_info, cells, kpoints, grid_count, kpt_count):
    count, width, slots, points = orbitals.shape
    pairs = grid_count * kpt_count
    pair_dev = grid_count
    lanes = NAO * pairs
    atoms = ATOM_DEV * grid_count
    lane_tile = min(2 * pairs, 128)
    return pl.pallas_call(
        functools.partial(whole_kernel, grid_count, kpt_count),
        grid=(count,),
        out_shape=jax.ShapeDtypeStruct((1, 2, NAO, ATOM_DEV, atoms * NAO), jnp.float32),
        in_specs=[
            pl.BlockSpec((1, width, slots, points), lambda b: (b, 0, 0, 0)),
            pl.BlockSpec((1, 1, points), lambda b: (b, 0, 0)),
            pl.BlockSpec((1, slots, slots), lambda b: (b, 0, 0)),
            pl.BlockSpec(mirror.shape, lambda b: (0, 0)),
            pl.BlockSpec(pair_info.shape, lambda b: (0, 0)),
            pl.BlockSpec(cells.shape, lambda b: (0, 0)),
            pl.BlockSpec(memory_space=pltpu.SMEM),
        ],
        out_specs=pl.BlockSpec((1, 2, NAO, ATOM_DEV, atoms * NAO), lambda b: (0, 0, 0, 0, 0)),
        scratch_shapes=[
            pltpu.VMEM((XP * slots, points), jnp.float32),
            pltpu.VMEM((slots * XP, points), jnp.bfloat16),
            pltpu.VMEM((HALF * 128, points), jnp.bfloat16),
            pltpu.VMEM((slots, 128), jnp.int32),
            pltpu.VMEM((6 * pair_dev, 128), jnp.int32),
            pltpu.VMEM((6 * pair_dev, 2 * HALF * XP), jnp.float32),
            pltpu.VMEM((12 * pair_dev, 128), jnp.float32),
            pltpu.VMEM((pair_dev, XP, 128), jnp.float32),
            pltpu.VMEM((grid_count * XP, 128), jnp.float32),
            pltpu.VMEM((kpt_count, 4 * grid_count, 128), jnp.float32),
            pltpu.VMEM((4 * pairs // lane_tile, 128, lane_tile), jnp.float32),
            pltpu.VMEM((XP, lanes), jnp.float32),
            pltpu.VMEM((atoms * NAO, lanes), jnp.bfloat16),
            pltpu.VMEM((2 * ATOM_DEV, lanes), jnp.float32),
            pltpu.SemaphoreType.DMA((grid_count,)),
            pltpu.SemaphoreType.DMA((grid_count,)),
            pltpu.SemaphoreType.DMA((kpt_count,)),
            pltpu.SemaphoreType.DMA((kpt_count,)),
        ],
        compiler_params=pltpu.CompilerParams(
            dimension_semantics=("arbitrary",),
            collective_id=0,
            has_side_effects=True,
            vmem_limit_bytes=60 * 1024 * 1024,
        ),
    )(orbitals, potential.reshape(count, 1, points), batch_pairs, mirror, pair_info, cells, kpoints)


def on_device(orbitals, potential, batch_pairs, pair_info, mirror, cell_table, kpoints):
    grid_count = lax.axis_size("grid")
    kpt_count = lax.axis_size("kpt")
    npairs = pair_info.shape[1]
    pair_dev = npairs // (grid_count * kpt_count)
    assert pair_dev == grid_count
    dense = whole(
        orbitals, potential, batch_pairs, mirror.reshape(1, -1), pair_info, cell_table.T, kpoints,
        grid_count, kpt_count,
    )
    return dense.transpose(0, 1, 3, 2, 4)


def solution(mesh):
    return jax.shard_map(
        on_device,
        mesh=mesh,
        in_specs=(
            P(("grid", "kpt"), None, None, None),
            P(("grid", "kpt"), None),
            P(("grid", "kpt"), None, None),
            P(),
            P(),
            P(),
            P("kpt", None),
        ),
        out_specs=P("kpt", None, "grid", None, None),
        check_vma=False,
    )
```

time: 44.9 us -> 29.3 us (0.65)
  Pallas kernels: 15.7 us -> 27.5 us
  local copies, waits for them, and re-layouts: 9.18 us -> 1.63 us
  starting transfers between devices: 7.25 us -> 0 us
  blocking collectives: 5.19 us -> 0 us
  waiting for transfers between devices: 4.97 us -> 0 us
  other arithmetic: 1.12 us -> 0 us
  matrix products: 0.83 us -> 0 us
    pallas_call x1, Pallas kernels: 15.7 us -> 27.5 us  [whole(): pl.pallas_call(functools.partial(whole_kernel, grid_count, kpt_count), gr...]
    all_to_all x1 -> x0, starting transfers between devices: 7.25 us -> none  [on_device(): got = lax.all_to_all(send, 'grid', split_axis=0, concat_axis=0, tiled=True)]
    all_gather x1 -> x0, blocking collectives: 5.19 us -> none  [on_device(): lax.all_gather(sym.reshape(NAO * NAO, 1, -1), 'kpt', axis=1, tiled=True)]
    all_to_all x1 -> x0, waiting for transfers between devices: 4.97 us -> none  [on_device(): got = lax.all_to_all(send, 'grid', split_axis=0, concat_axis=0, tiled=True)]
    reshape x4 -> x0, local copies, waits for them, and re-layouts: 2.27 us -> none  [the longest x1 1.93 us: phase_sum(): return dense.reshape(kpoints.shape[0], 2, ATOM_DEV, NAO, atoms * NAO)]
    gather x3 -> x0, local copies, waits for them, and re-layouts: 1.37 us -> none  [the longest x2 0.79 us: on_device(): ids = jnp.stack([pair_id(0), jnp.take(mirror, pair_id(half))])]
    transpose x3 -> x0, local copies, waits for them, and re-layouts: 0.98 us -> none  [the longest x1 0.68 us: phase_sum(): jnp.einsum('ksiabp,pj->ksiajb', weighted, col_hot, precision=lax.Precisio...]
    dot_general x2 -> x0, matrix products: 0.83 us -> none  [the longest x1 0.57 us: phase_sum(): jnp.einsum('ksiabp,pj->ksiajb', weighted, col_hot, precision=lax.Precisio...]
  transfers between devices with their start and end apart: 1 -> 0, of which waited for: 1 -> 0; matrix products, arithmetic and copies ran while one was open for 4% -> 0% of each run, Pallas kernels for 0% -> 0%
where the time goes in v4:
time: 29.3 us; the launch traced here: 29.2 us
  Pallas kernels  27.5 us (94%)
  local copies, waits for them, and re-layouts  1.63 us (6%)
    pallas_call x1, Pallas kernels, whole(): pl.pallas_call(functools.partial(whole_kernel, grid_count, kpt_count), gr...  27.5 us
    unnamed x1, local copies, waits for them, and re-layouts  1.63 us

profile of v4, /device:TPU:0, one launch (start us, length us, event | category | flops | bytes accessed | tf_op | source)
XLA Modules:
  0.0 29.2 jit_solution(8587363000018611940)
XLA Ops:
  0.0 27.5 %shard_map.73 = f32[1,2,13,4,416]{4,3,2,1,0:T(4,128)} custom-call(bf16[8,13,48,128]{3,2,1,0:T(8,128)(2,1)} %orb_ref.1, f32[8,1,128]{2,1,0:T(1,128)} %bitcast.5, s32[8,48,48]{2,1,0:T(8,128)} %pairs_ref.1, s32[1,256]{1,0:T(1,128)} %bitcast.7, s32[3,256]{1,0:T(4,128)} %info_ref.1, s32[3,61]{1,0:T(4,128)} %bitcast.6, f32[1,3]{1,0:T(1,128)} %kpt_ref.1), custom_call_target="tpu_custom_call" | custom-call | tf_op jit(solution)/shard_map/pallas_call | solution.py:262
  27.5 1.6 %copy.9 = f32[1,2,4,13,416]{4,2,3,1,0:T(4,128)} copy(f32[1,2,4,13,416]{4,2,3,1,0:T(4,128)} %bitcast.4) | data formatting | bytes 346112

commit v5 on v4

--- a/solution.py
+++ b/solution.py
@@ -14,6 +14,7 @@
 CP = 64
 ATOM_DEV = 4
 A_STEP = 8
+BATCH_STEP = 4
 
 two_pi = 2.0 * math.pi
 MESH = pl.DeviceIdType.MESH
@@ -58,41 +59,42 @@
                 at = (s * 2 + par) * pair_dev
                 ids[at : at + pair_dev, :] = (slot + first_pair(s - 1)) * 2 + par
 
-    weight = pot_ref[0]
-    for y in range(width):
-        vals = orb_ref[0, y].astype(jnp.float32)
-        base = (y % HALF) * 128 + (y // HALF) * CP
-        right[base : base + slots, :] = (vals * weight).astype(jnp.bfloat16)
-        rows_f32[y * slots : (y + 1) * slots, :] = vals
-    for a in range(slots):
-        left[a * XP : (a + 1) * XP, :] = rows_f32[pl.ds(a, XP, stride=slots), :].astype(jnp.bfloat16)
-    pairs = pairs_ref[0]
-    codes[:, 0:slots] = pairs * 2
-    codes[:, CP : CP + slots] = pairs * 2 + 1
-    wanted = ids[...]
-    for a0 in range(0, slots, A_STEP):
-        prod = lax.dot_general(
-            left[a0 * XP : (a0 + A_STEP) * XP, :], right[...], NT, preferred_element_type=jnp.float32
-        )
-        high = prod.astype(jnp.bfloat16)
-        low = (prod - high.astype(jnp.float32)).astype(jnp.bfloat16)
-        cols, hots = [], []
-        for a in range(A_STEP):
-            parts = [
-                part[a * XP : (a + 1) * XP, yp * 128 : (yp + 1) * 128]
-                for part in (high, low)
-                for yp in range(HALF)
-            ]
-            cols.append(jnp.concatenate(parts, axis=0))
-            hots.append(
-                (codes[a0 + a : a0 + a + 1, :] == wanted).astype(jnp.float32).astype(jnp.bfloat16)
-            )
-        acc[...] += lax.dot_general(
-            jnp.concatenate(hots, axis=1),
-            jnp.concatenate(cols, axis=1),
-            NT,
-            preferred_element_type=jnp.float32,
-        )
+    for b in range(BATCH_STEP):
+        weight = pot_ref[b]
+        for y in range(width):
+            vals = orb_ref[b, y].astype(jnp.float32)
+            base = (y % HALF) * 128 + (y // HALF) * CP
+            right[b, base : base + slots, :] = (vals * weight).astype(jnp.bfloat16)
+            rows_f32[b, y * slots : (y + 1) * slots, :] = vals
+        for a in range(slots):
+            left[b, a * XP : (a + 1) * XP, :] = rows_f32[b, pl.ds(a, XP, stride=slots), :].astype(jnp.bfloat16)
+        pairs = pairs_ref[b]
+        codes[b, :, 0:slots] = pairs * 2
+        codes[b, :, CP : CP + slots] = pairs * 2 + 1
+        wanted = ids[...]
+        for a0 in range(0, slots, A_STEP):
+            prod = lax.dot_general(
+                left[b, a0 * XP : (a0 + A_STEP) * XP, :], right[b], NT, preferred_element_type=jnp.float32
+            )
+            high = prod.astype(jnp.bfloat16)
+            low = (prod - high.astype(jnp.float32)).astype(jnp.bfloat16)
+            cols, hots = [], []
+            for a in range(A_STEP):
+                parts = [
+                    part[a * XP : (a + 1) * XP, yp * 128 : (yp + 1) * 128]
+                    for part in (high, low)
+                    for yp in range(HALF)
+                ]
+                cols.append(jnp.concatenate(parts, axis=0))
+                hots.append(
+                    (codes[b, a0 + a : a0 + a + 1, :] == wanted).astype(jnp.float32).astype(jnp.bfloat16)
+                )
+            acc[...] += lax.dot_general(
+                jnp.concatenate(hots, axis=1),
+                jnp.concatenate(cols, axis=1),
+                NT,
+                preferred_element_type=jnp.float32,
+            )
 
     @pl.when(step == pl.num_programs(0) - 1)
     def _():
@@ -261,12 +263,12 @@
     lane_tile = min(2 * pairs, 128)
     return pl.pallas_call(
         functools.partial(whole_kernel, grid_count, kpt_count),
-        grid=(count,),
+        grid=(count // BATCH_STEP,),
         out_shape=jax.ShapeDtypeStruct((1, 2, NAO, ATOM_DEV, atoms * NAO), jnp.float32),
         in_specs=[
-            pl.BlockSpec((1, width, slots, points), lambda b: (b, 0, 0, 0)),
-            pl.BlockSpec((1, 1, points), lambda b: (b, 0, 0)),
-            pl.BlockSpec((1, slots, slots), lambda b: (b, 0, 0)),
+            pl.BlockSpec((BATCH_STEP, width, slots, points), lambda b: (b, 0, 0, 0)),
+            pl.BlockSpec((BATCH_STEP, 1, points), lambda b: (b, 0, 0)),
+            pl.BlockSpec((BATCH_STEP, slots, slots), lambda b: (b, 0, 0)),
             pl.BlockSpec(mirror.shape, lambda b: (0, 0)),
             pl.BlockSpec(pair_info.shape, lambda b: (0, 0)),
             pl.BlockSpec(cells.shape, lambda b: (0, 0)),
@@ -274,10 +276,10 @@
         ],
         out_specs=pl.BlockSpec((1, 2, NAO, ATOM_DEV, atoms * NAO), lambda b: (0, 0, 0, 0, 0)),
         scratch_shapes=[
-            pltpu.VMEM((XP * slots, points), jnp.float32),
-            pltpu.VMEM((slots * XP, points), jnp.bfloat16),
-            pltpu.VMEM((HALF * 128, points), jnp.bfloat16),
-            pltpu.VMEM((slots, 128), jnp.int32),
+            pltpu.VMEM((BATCH_STEP, XP * slots, points), jnp.float32),
+            pltpu.VMEM((BATCH_STEP, slots * XP, points), jnp.bfloat16),
+            pltpu.VMEM((BATCH_STEP, HALF * 128, points), jnp.bfloat16),
+            pltpu.VMEM((BATCH_STEP, slots, 128), jnp.int32),
             pltpu.VMEM((6 * pair_dev, 128), jnp.int32),
             pltpu.VMEM((6 * pair_dev, 2 * HALF * XP), jnp.float32),
             pltpu.VMEM((12 * pair_dev, 128), jnp.float32),

time: 29.3 us -> 28.4 us (0.969)
  Pallas kernels: 27.5 us -> 26.6 us
    pallas_call x1, Pallas kernels: 27.5 us -> 26.6 us  [whole(): pl.pallas_call(functools.partial(whole_kernel, grid_count, kpt_count), gr...]
where the time goes in v5:
time: 28.4 us; the launch traced here: 28.3 us
  Pallas kernels  26.6 us (94%)
  local copies, waits for them, and re-layouts  1.63 us (6%)
    pallas_call x1, Pallas kernels, whole(): pl.pallas_call(functools.partial(whole_kernel, grid_count, kpt_count), gr...  26.6 us
    unnamed x1, local copies, waits for them, and re-layouts  1.63 us

profile of v5, /device:TPU:0, one launch (start us, length us, event | category | flops | bytes accessed | tf_op | source)
XLA Modules:
  0.0 28.3 jit_solution(9066043835276405350)
XLA Ops:
  0.0 26.6 %shard_map.73 = f32[1,2,13,4,416]{4,3,2,1,0:T(4,128)} custom-call(bf16[8,13,48,128]{3,2,1,0:T(8,128)(2,1)} %orb_ref.1, f32[8,1,128]{2,1,0:T(1,128)} %bitcast.5, s32[8,48,48]{2,1,0:T(8,128)} %pairs_ref.1, s32[1,256]{1,0:T(1,128)} %bitcast.7, s32[3,256]{1,0:T(4,128)} %info_ref.1, s32[3,61]{1,0:T(4,128)} %bitcast.6, f32[1,3]{1,0:T(1,128)} %kpt_ref.1), custom_call_target="tpu_custom_call" | custom-call | tf_op jit(solution)/shard_map/pallas_call | solution.py:264
  26.6 1.6 %copy.9 = f32[1,2,4,13,416]{4,2,3,1,0:T(4,128)} copy(f32[1,2,4,13,416]{4,2,3,1,0:T(4,128)} %bitcast.4) | data formatting | bytes 346112
